TPU v7x, 512 devices: a whole 4x8x8 slice. The times are simulated.
512 devices in a mesh: seq: 64 (over y_lo, z, core), chan: 8 (over x, y_hi).
Axes of the slice: x: 4, y: 8 (y_hi: 2, y_lo: 4; y = y_hi * 4 + y_lo), z: 8, core: 2. Of those that a mesh axis runs over, the one named last changes fastest.
Arguments:
- gate_in: bfloat16 [8192, 4096], P('seq', 'chan'), may hold values from -40 to 40
- key_in: bfloat16 [8192, 4096], P('seq', 'chan'), may hold values from -6 to 6
- value_in: bfloat16 [8192, 4096], P('seq', 'chan'), may hold values from -6 to 6
- out_grad: bfloat16 [8192, 4096], P('seq', 'chan'), may hold values from -6 to 6
- residue: float32 [16, 4096], P(None, 'chan'), may hold values from -4 to 4
- log_rate: float32 [16, 4096], P(None, 'chan'), may hold values from -14 to -3
- skip: float32 [4096], P('chan'), may hold values from -4 to 4
Outputs:
- gated_out: bfloat16 [8192, 4096], P('seq', 'chan')
- gate_grad: bfloat16 [8192, 4096], P('seq', 'chan')
- key_grad: bfloat16 [8192, 4096], P('seq', 'chan')
- value_grad: bfloat16 [8192, 4096], P('seq', 'chan')
- residue_grad: float32 [16, 4096], P(None, 'chan')
- log_rate_grad: float32 [16, 4096], P(None, 'chan')
- skip_grad: float32 [4096], P('chan')
All inputs are finite; a program needn't handle non-finite values.
Results may differ from a plain program's by a relative error of at most 0.002.
Values sent between devices are 32-bit elements; how exact they have to be, the bound alone decides.
No kernel may reach another device: no remote copies, remote signals or barrier semaphores. Data moves between devices by JAX's collectives and lax.ppermute only.
A program may use at most 64 MiB of HBM per device.

v0:
```python
import math

import jax
import jax.numpy as jnp
from jax import lax
from jax.sharding import PartitionSpec as P

CLIP_RMS = 1.0
FULL_PRECISION = lax.Precision.HIGHEST


def owned_frequency(seq_count, row_count, device):
    parity = jnp.arange(2, dtype=jnp.int32)[:, None]
    second = jnp.arange(row_count, dtype=jnp.int32)[None, :]
    return 2 * device + parity + 2 * seq_count * second


def local_phase(seq_count, row_count, device):
    fft_size = 2 * seq_count * row_count
    frequency = owned_frequency(seq_count, row_count, device)[:, :, None]
    column = jnp.arange(row_count, dtype=jnp.int32)[None, None, :]
    phase_turns = frequency * column % fft_size
    angles = phase_turns.astype(jnp.float32) * (2.0 * math.pi / fft_size)
    return (jnp.cos(angles), jnp.sin(angles))


def cross_phase(seq_count):
    parity = jnp.arange(2, dtype=jnp.int32)[:, None, None]
    target = jnp.arange(seq_count, dtype=jnp.int32)[None, :, None]
    source = jnp.arange(seq_count, dtype=jnp.int32)[None, None, :]
    phase_turns = source * (2 * target + parity) % (2 * seq_count)
    angles = phase_turns.astype(jnp.float32) * (math.pi / seq_count)
    return (jnp.cos(angles), jnp.sin(angles))


def forward_spectrum(fields, tables):
    cos_local, sin_local, cos_cross, sin_cross = tables
    field_count, row_count, channel_count = fields.shape
    seq_count = lax.axis_size("seq")
    block_rows = row_count // seq_count
    columns = lax.all_to_all(fields, "seq", split_axis=1, concat_axis=1, tiled=True)
    columns = columns.reshape(field_count, seq_count, block_rows, channel_count)
    cross_re = jnp.einsum("ems,fsjc->emfjc", cos_cross, columns, precision=FULL_PRECISION)
    cross_im = -jnp.einsum("ems,fsjc->emfjc", sin_cross, columns, precision=FULL_PRECISION)
    pair_re, pair_im = (
        lax.all_to_all(cross_re, "seq", split_axis=1, concat_axis=3, tiled=True),
        lax.all_to_all(cross_im, "seq", split_axis=1, concat_axis=3, tiled=True),
    )
    pair_re = pair_re.reshape(2, field_count, row_count, channel_count)
    pair_im = pair_im.reshape(2, field_count, row_count, channel_count)
    spec_re = jnp.einsum(
        "ekj,efjc->efkc", cos_local, pair_re, precision=FULL_PRECISION
    ) + jnp.einsum("ekj,efjc->efkc", sin_local, pair_im, precision=FULL_PRECISION)
    spec_im = jnp.einsum(
        "ekj,efjc->efkc", cos_local, pair_im, precision=FULL_PRECISION
    ) - jnp.einsum("ekj,efjc->efkc", sin_local, pair_re, precision=FULL_PRECISION)
    return (spec_re, spec_im)


def inverse_fields(spec_re, spec_im, tables):
    cos_local, sin_local, cos_cross, sin_cross = tables
    field_count, row_count, channel_count = (spec_re.shape[1], spec_re.shape[2], spec_re.shape[3])
    seq_count = lax.axis_size("seq")
    block_rows = row_count // seq_count
    fft_size = 2 * seq_count * row_count
    back_re = jnp.einsum(
        "ekj,efkc->efjc", cos_local, spec_re, precision=FULL_PRECISION
    ) - jnp.einsum("ekj,efkc->efjc", sin_local, spec_im, precision=FULL_PRECISION)
    back_im = jnp.einsum(
        "ekj,efkc->efjc", cos_local, spec_im, precision=FULL_PRECISION
    ) + jnp.einsum("ekj,efkc->efjc", sin_local, spec_re, precision=FULL_PRECISION)
    back_re = back_re.reshape(2, field_count, seq_count, block_rows, channel_count)
    back_im = back_im.reshape(2, field_count, seq_count, block_rows, channel_count)
    blocks_re, blocks_im = (
        lax.all_to_all(back_re, "seq", split_axis=2, concat_axis=2, tiled=True),
        lax.all_to_all(back_im, "seq", split_axis=2, concat_axis=2, tiled=True),
    )
    values = (
        jnp.einsum("ems,efmjc->fsjc", cos_cross, blocks_re, precision=FULL_PRECISION)
        - jnp.einsum("ems,efmjc->fsjc", sin_cross, blocks_im, precision=FULL_PRECISION)
    ) / fft_size
    rows_back = lax.all_to_all(values, "seq", split_axis=1, concat_axis=2, tiled=True)
    return rows_back.reshape(field_count, row_count, channel_count)


def closed_spectrum(amplitude, decay_rate, seq_count, row_count, device):
    fft_size = 2 * seq_count * row_count
    length = fft_size // 2
    frequency = owned_frequency(seq_count, row_count, device)
    signed_freq = jnp.where(2 * frequency >= fft_size, frequency - fft_size, frequency)
    angles = signed_freq.astype(jnp.float32) * (2.0 * math.pi / fft_size)
    sine_table = jnp.sin(angles)[:, :, None]
    half_sine = jnp.sin(0.5 * angles)
    double_half = (2.0 * half_sine * half_sine)[:, :, None]
    alternate = (1 - 2 * (frequency % 2)).astype(jnp.float32)[:, :, None]
    mode_step = jnp.exp(-decay_rate)
    mode_base = -jnp.expm1(-decay_rate)
    mode_tail = jnp.exp(-decay_rate * length)

    def add_mode(mode_index, partial_value):
        acc_re, acc_im = partial_value
        decay_step = mode_step[mode_index][None, None, :]
        den_re = mode_base[mode_index][None, None, :] + decay_step * double_half
        den_im = decay_step * sine_table
        numerator = 1.0 - alternate * mode_tail[mode_index][None, None, :]
        weight = (
            amplitude[mode_index][None, None, :] * numerator / (den_re * den_re + den_im * den_im)
        )
        return (acc_re + weight * den_re, acc_im - weight * den_im)

    empty_acc = jnp.zeros((2, row_count, amplitude.shape[1]), jnp.float32)
    return lax.fori_loop(0, amplitude.shape[0], add_mode, (empty_acc, empty_acc))


def per_device(gate_in, key_in, value_in, out_grad, residue, log_rate, skip):
    row_count, channel_count = gate_in.shape
    seq_count = lax.axis_size("seq")
    device = lax.axis_index("seq")
    mode_count = residue.shape[0]
    decay_rate = jnp.exp(log_rate)
    unit_scale = jnp.sqrt(2.0 * decay_rate / mode_count)
    amplitude = residue * unit_scale
    positions = (device * row_count + jnp.arange(row_count, dtype=jnp.int32)).astype(jnp.float32)
    cos_local, sin_local = local_phase(seq_count, row_count, device)
    cos_cross, sin_cross = cross_phase(seq_count)
    tables = (cos_local, sin_local, cos_cross, sin_cross)
    gate_field = gate_in.astype(jnp.float32)
    mixed_field = key_in.astype(jnp.float32) * value_in.astype(jnp.float32)
    gated_slope = out_grad.astype(jnp.float32) * gate_field
    base_fields = mixed_field[None]
    spec_re, spec_im = forward_spectrum(base_fields, tables)
    mix_re, mix_im = (spec_re[:, 0], spec_im[:, 0])
    filt_re, filt_im = closed_spectrum(amplitude, decay_rate, seq_count, row_count, device)
    prod_re = mix_re * filt_re - mix_im * filt_im
    prod_im = mix_re * filt_im + mix_im * filt_re
    convolved = inverse_fields(prod_re[:, None], prod_im[:, None], tables)[0]
    slope_spec_re, slope_spec_im = forward_spectrum(gated_slope[None], tables)
    slope_re = slope_spec_re[:, 0]
    slope_im = slope_spec_im[:, 0]
    back_re = filt_re * slope_re + filt_im * slope_im
    back_im = filt_re * slope_im - filt_im * slope_re
    tap_re = mix_re * slope_re + mix_im * slope_im
    tap_im = mix_re * slope_im - mix_im * slope_re
    back_re, back_im, tap_re, tap_im = (back_re, back_im, tap_re, tap_im)
    inverse_out = inverse_fields(
        jnp.stack([back_re, tap_re], axis=1), jnp.stack([back_im, tap_im], axis=1), tables
    )
    back_field, tap_grad = (inverse_out[0], inverse_out[1])
    filtered = convolved + skip[None, :] * mixed_field
    gated_out = (gate_field * filtered).astype(jnp.bfloat16)
    gate_grad = (out_grad.astype(jnp.float32) * filtered).astype(jnp.bfloat16)
    mixed_grad = back_field + skip[None, :] * gated_slope
    key_grad = (mixed_grad * value_in.astype(jnp.float32)).astype(jnp.bfloat16)
    value_grad = (mixed_grad * key_in.astype(jnp.float32)).astype(jnp.bfloat16)
    timed_grad = tap_grad * positions[:, None]

    def mode_sums(mode_items):
        mode_rate, mode_unit, mode_amp = mode_items
        envelope = jnp.exp(-mode_rate[None, :] * positions[:, None])
        plain_sum = jnp.sum(tap_grad * envelope, axis=0)
        timed_sum = jnp.sum(timed_grad * envelope, axis=0)
        res_term = plain_sum * mode_unit
        log_term = (0.5 * plain_sum - mode_rate * timed_sum) * mode_amp
        return (res_term, log_term)

    part_res, part_log = lax.map(mode_sums, (decay_rate, unit_scale, amplitude))
    part_skip = jnp.sum(gated_slope * mixed_field, axis=0)
    raw_res, raw_log, raw_skip = lax.psum((part_res, part_log, part_skip), "seq")
    local_squares = (
        jnp.sum(raw_res * raw_res) + jnp.sum(raw_log * raw_log) + jnp.sum(raw_skip * raw_skip)
    )
    total_squares = lax.psum(local_squares, "chan")
    root_mean = jnp.sqrt(
        total_squares / ((2 * mode_count + 1) * channel_count * lax.axis_size("chan"))
    )
    factor = CLIP_RMS / jnp.maximum(root_mean, CLIP_RMS)
    return (
        gated_out,
        gate_grad,
        key_grad,
        value_grad,
        raw_res * factor,
        raw_log * factor,
        raw_skip * factor,
    )


def solution(mesh):
    return jax.shard_map(
        per_device,
        mesh=mesh,
        in_specs=(
            P("seq", "chan"),
            P("seq", "chan"),
            P("seq", "chan"),
            P("seq", "chan"),
            P(None, "chan"),
            P(None, "chan"),
            P("chan"),
        ),
        out_specs=(
            P("seq", "chan"),
            P("seq", "chan"),
            P("seq", "chan"),
            P("seq", "chan"),
            P(None, "chan"),
            P(None, "chan"),
            P("chan"),
        ),
        check_vma=False,
    )
```

profile of v0, /device:TPU:2, one launch (start us, length us, event | category | flops | bytes accessed | tf_op | source)
XLA Modules:
  0.0 879.9 jit_solution(5300767621150201152)
XLA Ops:
  9.1 14.5 %all-to-all-start.6 = ((f32[1,128,512]{2,0,1:T(1,128)}), f32[1,128,512]{2,0,1:T(1,128)S(1)}, u32[]{:S(2)}, u32[]{:S(2)}) async-start(f32[1,128,512]{2,0,1:T(1,128)} %copy.127), calls=%async_computation.6 | async-start | bytes 524288 | tf_op jit(solution)/shard_map/all_to_all | solution.py:41
  24.7 11.4 %all-to-all-done.6 = f32[1,128,512]{2,0,1:T(1,128)S(1)} async-done(((f32[1,128,512]{2,0,1:T(1,128)}), f32[1,128,512]{2,0,1:T(1,128)S(1)}, u32[]{:S(2)}, u32[]{:S(2)}) %all-to-all-start.6) | async-done | bytes 262176 | tf_op jit(solution)/shard_map/all_to_all | solution.py:41
  36.1 5.2 all-to-all-start
  44.2 9.6 %all-to-all-done = f32[1,128,512]{2,0,1:T(1,128)S(1)} async-done(((f32[1,128,512]{2,0,1:T(1,128)}), f32[1,128,512]{2,0,1:T(1,128)S(1)}, u32[]{:S(2)}, u32[]{:S(2)}) %all-to-all-start) | async-done | bytes 262176 | tf_op jit(solution)/shard_map/all_to_all | solution.py:41
  53.8 5.2 all-to-all-start.7
  61.0 15.0 %all-to-all-done.7 = f32[2,64,1,2,512]{4,3,0,2,1:T(2,128)S(1)} async-done(((f32[2,64,1,2,512]{4,3,0,2,1:T(2,128)}), f32[2,64,1,2,512]{4,3,0,2,1:T(2,128)S(1)}, u32[]{:S(2)}, u32[]{:S(2)}) %all-to-all-start.7) | async-done | bytes 524320 | tf_op jit(solution)/shard_map/all_to_all | solution.py:46
  76.0 6.3 all-to-all-start.8
  85.3 14.1 %all-to-all-done.8 = f32[2,64,1,2,512]{4,3,0,2,1:T(2,128)S(1)} async-done(((f32[2,64,1,2,512]{4,3,0,2,1:T(2,128)}), f32[2,64,1,2,512]{4,3,0,2,1:T(2,128)S(1)}, u32[]{:S(2)}, u32[]{:S(2)}) %all-to-all-start.8) | async-done | bytes 524320 | tf_op jit(solution)/shard_map/all_to_all | solution.py:47
  99.4 6.4 all-to-all-start.2
  105.8 11.2 %while.32 = (s32[]{:T(128)}, f32[2,128,512]{2,1,0:T(8,128)S(1)}, f32[2,128,512]{2,1,0:T(8,128)S(1)}, f32[16,512]{1,0:T(8,128)S(1)}, f32[16,512]{1,0:T(8,128)S(1)...) while((s32[]{:T(128)}, f32[2,128,512]{2,1,0:T(8,128)S(1)}, ...), condition=%wide.region_1.2_spmd.clone.clone.clone, body=%wide.region_0.1_spmd.clone.clone.clone.sunk | while | flops 2103555 | bytes 2129047 | solution.py:112
  119.1 3.9 all-to-all-done.2
  123.8 7.2 all-to-all-start.1
  139.7 8.3 all-to-all-done.1
  147.9 2.1 copy.101
  154.5 2.3 fusion.43
  159.1 9.6 %fusion.22 = f32[2,1,128,512]{3,2,0,1:T(8,128)S(1)} fusion(f32[2,512,128]{1,2,0:T(8,128)S(1)} %fusion.93, f32[2,128,512]{1,2,0:T(8,128)S(1)} %get-tuple-element.411, s32[2,128]{1,0:T(2,128)S(1)} %broadcast_add_fusion), kind=kOutput, calls=%fused_computation.54 | convolution fusion | flops 201916416 | bytes 1573888 | tf_op jit(solution)/shard_map/ekj,efkc->efjc/dot_general | solution.py:71
  169.9 6.2 all-to-all-start.4
  179.5 13.6 %all-to-all-done.4 = f32[2,1,64,2,512]{4,0,3,1,2:T(2,128)S(1)} async-done(((f32[2,1,64,2,512]{4,0,3,1,2:T(2,128)}), f32[2,1,64,2,512]{4,0,3,1,2:T(2,128)S(1)}, u32[]{:S(2)}, u32[]{:S(2)}) %all-to-all-start.4) | async-done | bytes 524320 | tf_op jit(solution)/shard_map/all_to_all | solution.py:76
  193.9 6.4 all-to-all-start.3
  206.5 3.0 copy.154
  209.5 7.8 all-to-all-done.3
  217.3 6.4 all-to-all-start.10
  229.2 22.8 %all-to-all-done.10 = f32[2,2,64,2,512]{4,0,3,1,2:T(2,128)S(1)} async-done(((f32[2,2,64,2,512]{4,0,3,1,2:T(2,128)}), f32[2,2,64,2,512]{4,0,3,1,2:T(2,128)S(1)}, u32[]{:S(2)}, u32[]{:S(2)}) %all-to-all-start.10) | async-done | bytes 1048608 | tf_op jit(solution)/shard_map/all_to_all | solution.py:76
  252.0 6.2 all-to-all-start.9
  261.7 24.9 %all-to-all-done.9 = f32[2,2,64,2,512]{4,0,3,1,2:T(2,128)S(1)} async-done(((f32[2,2,64,2,512]{4,0,3,1,2:T(2,128)}), f32[2,2,64,2,512]{4,0,3,1,2:T(2,128)S(1)}, u32[]{:S(2)}, u32[]{:S(2)}) %all-to-all-start.9) | async-done | bytes 1048608 | tf_op jit(solution)/shard_map/all_to_all | solution.py:75
  286.5 6.2 all-to-all-start.5
  296.9 8.3 all-to-all-done.5
  305.2 5.2 all-to-all-start.11
  310.7 16.8 %all-to-all-done.11 = f32[2,64,2,512]{3,2,0,1:T(2,128)S(1)} async-done(((f32[2,64,2,512]{3,2,0,1:T(2,128)}), f32[2,64,2,512]{3,2,0,1:T(2,128)S(1)}, u32[]{:S(2)}, u32[]{:S(2)}) %all-to-all-start.11) | async-done | bytes 524320 | tf_op jit(solution)/shard_map/all_to_all | solution.py:82
  328.0 46.0 %while.31 = (s32[]{:T(128)}, f32[16,512]{1,0:T(8,128)}, f32[16,512]{1,0:T(8,128)}, f32[16,512]{1,0:T(8,128)S(1)}, f32[128,512]{1,0:T(8,128)S(1)}, /*index=5*/f32...) while((s32[]{:T(128)}, f32[16,512]{1,0:T(8,128)}, ...), condition=%wide.region_5.6_spmd.clone, body=%wide.region_2.5_spmd.clone.sunk | while | flops 329986 | bytes 558217 | solution.py:166
  375.6 460.1 %all-reduce.3.cloned.1.call-done = (f32[16,512]{1,0:T(8,128)}, f32[16,512]{1,0:T(8,128)}, f32[512]{0:T(512)}) async-done(((f32[16,512]{1,0:T(8,128)}, f32[16,512]{1,0:T(8,128)}, f32[512]{0:T(512)}), (f32[16,512]{1,0:T(8,128)}, f32[16,512]{1,0:T(8,128)}, f32[512]{0:T(512)})) %all-reduce.3.cloned.1.call-update) | async-done | bytes 67600 | tf_op jit(solution)/shard_map/psum | solution.py:168
  840.4 29.8 %psum.31 = f32[]{:T(128)} all-reduce(f32[]{:T(128)S(6)} %add.339), channel_id=1, replica_groups=mesh['seq'=64,'chan'=8] {'chan'}, use_global_device_ids=true, to_apply=%region_13.14 | all-reduce | flops 1 | bytes 8 | tf_op jit(solution)/shard_map/psum | solution.py:172
  (289 shorter events, 116.8 us)
Async XLA Ops:
  9.1 14.5 %copy-start.10 = (bf16[128,512]{1,0:T(8,128)(2,1)S(1)}, bf16[128,512]{1,0:T(8,128)(2,1)}, u32[]{:S(2)}) copy-start(bf16[128,512]{1,0:T(8,128)(2,1)} %param.13) | copy-start | bytes 393220
  9.1 14.5 %copy-start.11 = (bf16[128,512]{1,0:T(8,128)(2,1)S(1)}, bf16[128,512]{1,0:T(8,128)(2,1)}, u32[]{:S(2)}) copy-start(bf16[128,512]{1,0:T(8,128)(2,1)} %param.12) | copy-start | bytes 393220
  9.1 27.0 %all-to-all-start.6 = ((f32[1,128,512]{2,0,1:T(1,128)}), f32[1,128,512]{2,0,1:T(1,128)S(1)}, u32[]{:S(2)}, u32[]{:S(2)}) async-start(f32[1,128,512]{2,0,1:T(1,128)} %copy.127), calls=%async_computation.6 | async-start | bytes 524288 | tf_op jit(solution)/shard_map/all_to_all | solution.py:41
  36.1 17.6 %all-to-all-start = ((f32[1,128,512]{2,0,1:T(1,128)}), f32[1,128,512]{2,0,1:T(1,128)S(1)}, u32[]{:S(2)}, u32[]{:S(2)}) async-start(f32[1,128,512]{2,0,1:T(1,128)} %copy.97), calls=%async_computation | async-start | bytes 524288 | tf_op jit(solution)/shard_map/all_to_all | solution.py:41
  53.8 22.2 %all-to-all-start.7 = ((f32[2,64,1,2,512]{4,3,0,2,1:T(2,128)}), f32[2,64,1,2,512]{4,3,0,2,1:T(2,128)S(1)}, u32[]{:S(2)}, u32[]{:S(2)}) async-start(f32[2,64,1,2,512]{4,3,0,2,1:T(2,128)} %copy.130), calls=%async_computation.7 | async-start | bytes 1048576 | tf_op jit(solution)/shard_map/all_to_all | solution.py:46
  76.0 6.3 copy-start.14
  76.0 6.4 copy-start.15
  76.0 23.4 %all-to-all-start.8 = ((f32[2,64,1,2,512]{4,3,0,2,1:T(2,128)}), f32[2,64,1,2,512]{4,3,0,2,1:T(2,128)S(1)}, u32[]{:S(2)}, u32[]{:S(2)}) async-start(f32[2,64,1,2,512]{4,3,0,2,1:T(2,128)} %copy.136), calls=%async_computation.8 | async-start | bytes 1048576 | tf_op jit(solution)/shard_map/all_to_all | solution.py:47
  99.4 23.6 %all-to-all-start.2 = ((f32[2,64,1,2,512]{4,3,0,2,1:T(2,128)}), f32[2,64,1,2,512]{4,3,0,2,1:T(2,128)S(1)}, u32[]{:S(2)}, u32[]{:S(2)}) async-start(f32[2,64,1,2,512]{4,3,0,2,1:T(2,128)} %copy.106), calls=%async_computation.2 | async-start | bytes 1048576 | tf_op jit(solution)/shard_map/all_to_all | solution.py:47
  123.0 0.8 copy-start.1
  123.8 24.1 %all-to-all-start.1 = ((f32[2,64,1,2,512]{4,3,0,2,1:T(2,128)}), f32[2,64,1,2,512]{4,3,0,2,1:T(2,128)}, u32[]{:S(2)}, u32[]{:S(2)}) async-start(f32[2,64,1,2,512]{4,3,0,2,1:T(2,128)} %copy.100), calls=%async_computation.1 | async-start | bytes 1048576 | tf_op jit(solution)/shard_map/all_to_all | solution.py:46
  133.1 1.0 copy-start.2
  151.3 1.1 copy-start.5
  154.5 2.3 copy-start
  169.9 23.2 %all-to-all-start.4 = ((f32[2,1,64,2,512]{4,0,3,1,2:T(2,128)}), f32[2,1,64,2,512]{4,0,3,1,2:T(2,128)S(1)}, u32[]{:S(2)}, u32[]{:S(2)}) async-start(f32[2,1,64,2,512]{4,0,3,1,2:T(2,128)} %bitcast.28), calls=%async_computation.4 | async-start | bytes 1048576 | tf_op jit(solution)/shard_map/all_to_all | solution.py:76
  193.1 0.8 copy-start.3
  193.1 7.2 copy-start.6
  193.1 7.2 copy-start.7
  193.9 23.3 %all-to-all-start.3 = ((f32[2,1,64,2,512]{4,0,3,1,2:T(2,128)}), f32[2,1,64,2,512]{4,0,3,1,2:T(2,128)}, u32[]{:S(2)}, u32[]{:S(2)}) async-start(f32[2,1,64,2,512]{4,0,3,1,2:T(2,128)} %bitcast.21), calls=%async_computation.3 | async-start | bytes 1048576 | tf_op jit(solution)/shard_map/all_to_all | solution.py:75
  217.3 34.7 %all-to-all-start.10 = ((f32[2,2,64,2,512]{4,0,3,1,2:T(2,128)}), f32[2,2,64,2,512]{4,0,3,1,2:T(2,128)S(1)}, u32[]{:S(2)}, u32[]{:S(2)}) async-start(f32[2,2,64,2,512]{4,0,3,1,2:T(2,128)} %copy.154), calls=%async_computation.10 | async-start | bytes 2097152 | tf_op jit(solution)/shard_map/all_to_all | solution.py:76
  229.2 29.0 %copy-start.4 = (f32[2,1,64,2,512]{4,0,3,1,2:T(2,128)S(1)}, f32[2,1,64,2,512]{4,0,3,1,2:T(2,128)}, u32[]{:S(2)}) copy-start(f32[2,1,64,2,512]{4,0,3,1,2:T(2,128)} %copy-done.3) | copy-start | bytes 1572868
  252.0 34.5 %all-to-all-start.9 = ((f32[2,2,64,2,512]{4,0,3,1,2:T(2,128)}), f32[2,2,64,2,512]{4,0,3,1,2:T(2,128)S(1)}, u32[]{:S(2)}, u32[]{:S(2)}) async-start(f32[2,2,64,2,512]{4,0,3,1,2:T(2,128)} %copy.150), calls=%async_computation.9 | async-start | bytes 2097152 | tf_op jit(solution)/shard_map/all_to_all | solution.py:75
  286.5 18.7 %all-to-all-start.5 = ((f32[1,64,2,512]{3,2,0,1:T(2,128)}), f32[1,64,2,512]{3,2,0,1:T(2,128)S(1)}, u32[]{:S(2)}, u32[]{:S(2)}) async-start(f32[1,64,2,512]{3,2,0,1:T(2,128)} %copy.126), calls=%async_computation.5 | async-start | bytes 524288 | tf_op jit(solution)/shard_map/all_to_all | solution.py:82
  305.2 22.2 %all-to-all-start.11 = ((f32[2,64,2,512]{3,2,0,1:T(2,128)}), f32[2,64,2,512]{3,2,0,1:T(2,128)S(1)}, u32[]{:S(2)}, u32[]{:S(2)}) async-start(f32[2,64,2,512]{3,2,0,1:T(2,128)} %copy.156), calls=%async_computation.11 | async-start | bytes 1048576 | tf_op jit(solution)/shard_map/all_to_all | solution.py:82
  310.4 525.3 %all-reduce.3.cloned.1.call-start = ((), (), s32[]{:S(2)}) async-start(), calls=%async_computation.12 | async-start | bytes 135168 | tf_op jit(solution)/shard_map/psum | solution.py:168
  328.0 46.0 %copy-start.8 = (bf16[128,512]{1,0:T(8,128)(2,1)S(1)}, bf16[128,512]{1,0:T(8,128)(2,1)}, u32[]{:S(2)}) copy-start(bf16[128,512]{1,0:T(8,128)(2,1)} %param.14) | copy-start | bytes 393220
  328.0 46.0 %copy-start.9 = (bf16[128,512]{1,0:T(8,128)(2,1)S(1)}, bf16[128,512]{1,0:T(8,128)(2,1)}, u32[]{:S(2)}) copy-start(bf16[128,512]{1,0:T(8,128)(2,1)} %param.11) | copy-start | bytes 393220
  328.0 46.0 %copy-start.17 = (f32[512]{0:T(512)S(1)}, f32[512]{0:T(512)}, u32[]{:S(2)}) copy-start(f32[512]{0:T(512)} %param.17) | copy-start | bytes 6148
  835.7 1.4 copy-start.12
  837.1 33.8 %copy-start.13 = (f32[16,512]{1,0:T(8,128)S(1)}, f32[16,512]{1,0:T(8,128)}, u32[]{:S(2)}) copy-start(f32[16,512]{1,0:T(8,128)} %get-tuple-element.391) | copy-start | bytes 98308
  837.1 0.7 copy-start.16
Sparse Core Ops, SparseCore 0:
  375.8 459.9 all-reduce.2
where the time goes:
time: 892 us; the launch traced here: 880 us
  waiting for transfers between devices  617 us (69%)
  starting transfers between devices  81.3 us (9%)
  local copies, waits for them, and re-layouts  71.2 us (8%)
  matrix products  38.6 us (4%)
  blocking collectives  29.8 us (3%)
  other arithmetic  23.9 us (3%)
  between operations  17.7 us (2%)
    psum x1, waiting for transfers between devices, per_device(): lax.psum((part_res, part_log, part_skip), 'seq')  460 us
    dynamic_update_slice x32, local copies, waits for them, and re-layouts, per_device(): part_res, part_log = lax.map(mode_sums, (decay_rate, unit_scale, amplitude))  42.9 us
    all_to_all x2, waiting for transfers between devices, inverse_fields(): lax.all_to_all(back_im, 'seq', split_axis=2, concat_axis=2, tiled=True)  36.4 us
    all_to_all x2, waiting for transfers between devices, inverse_fields(): lax.all_to_all(back_re, 'seq', split_axis=2, concat_axis=2, tiled=True)  32.6 us
    psum x1, blocking collectives, per_device(): total_squares = lax.psum(local_squares, 'chan')  29.8 us
    all_to_all x2, waiting for transfers between devices, inverse_fields(): lax.all_to_all(values, 'seq', split_axis=1, concat_axis=2, tiled=True)  25.1 us
    all_to_all x2, waiting for transfers between devices, forward_spectrum(): lax.all_to_all(cross_re, 'seq', split_axis=1, concat_axis=3, tiled=True)  23.2 us
    all_to_all x2, waiting for transfers between devices, forward_spectrum(): lax.all_to_all(fields, 'seq', split_axis=1, concat_axis=1, tiled=True)  21 us
  transfers between devices with their start and end apart: 13, of which 13 were waited for; matrix products, arithmetic and copies ran while one was open for 6% of the time, Pallas kernels for 0%

commit v1 on v0

v1 whole, which is shorter than its diff:
```python
import functools

import jax
import jax.numpy as jnp
from jax import lax
from jax.experimental import pallas as pl
from jax.experimental.pallas import tpu as pltpu
from jax.sharding import PartitionSpec as P

CLIP_RMS = 1.0
LANES = 128
SUBLANES = 8
ROWS_OUT = 8
ROWS_BACK = 8
VMEM = pl.BlockSpec(memory_space=pltpu.VMEM)
PARAMS = pltpu.CompilerParams(vmem_limit_bytes=32 * 1024 * 1024)


def tile_of(ref, chunk, group):
    return ref[pl.ds(pl.multiple_of(chunk * SUBLANES, SUBLANES), SUBLANES), group * LANES : (group + 1) * LANES]


def spread(tile, row):
    return jnp.broadcast_to(tile[row : row + 1], (SUBLANES, LANES))


def summary_kernel(key_ref, value_ref, gate_ref, grad_ref, rate_ref, out_ref, mixed, slope):
    block, width = key_ref.shape
    modes = rate_ref.shape[0]
    halves, groups = modes // SUBLANES, width // LANES
    mixed[...] = key_ref[...].astype(jnp.float32) * value_ref[...].astype(jnp.float32)
    slope[...] = grad_ref[...].astype(jnp.float32) * gate_ref[...].astype(jnp.float32)
    steps = {}
    for half in range(halves):
        for group in range(groups):
            rate = jnp.exp(rate_ref[half * SUBLANES : (half + 1) * SUBLANES, group * LANES : (group + 1) * LANES])
            steps[half, group] = jnp.exp(-rate)
    zero = jnp.zeros((SUBLANES, LANES), jnp.float32)
    keys = [(half, group) for half in range(halves) for group in range(groups)]

    def advance(chunk, carry):
        carry = list(carry)
        x_tiles = [tile_of(mixed, chunk, group) for group in range(groups)]
        z_tiles = [tile_of(slope, chunk, group) for group in range(groups)]
        back_tiles = [tile_of(slope, block // SUBLANES - 1 - chunk, group) for group in range(groups)]
        for inner in range(SUBLANES):
            x_rows = [spread(tile, inner) for tile in x_tiles]
            z_rows = [spread(tile, inner) for tile in z_tiles]
            back_rows = [spread(tile, SUBLANES - 1 - inner) for tile in back_tiles]
            for at, (half, group) in enumerate(keys):
                state, timed, plain_sum, timed_sum, back, back_timed = carry[at]
                step = steps[half, group]
                moved = step * state
                timed = step * timed + moved
                state = moved + x_rows[group]
                plain_sum = plain_sum + z_rows[group] * state
                timed_sum = timed_sum + z_rows[group] * timed
                back_moved = step * back
                back_timed = step * back_timed + back_moved
                back = back_moved + back_rows[group]
                carry[at] = (state, timed, plain_sum, timed_sum, back, back_timed)
        return tuple(carry)

    done = lax.fori_loop(0, block // SUBLANES, advance, tuple((zero,) * 6 for _ in keys))
    for at, (half, group) in enumerate(keys):
        state, timed, plain_sum, timed_sum, back, back_timed = done[at]
        step = steps[half, group]
        base = (group * modes + half * SUBLANES) * ROWS_OUT
        lanes = slice(group * LANES, (group + 1) * LANES)
        skip_part = jnp.sum(mixed[:, lanes] * slope[:, lanes], axis=0, keepdims=True)
        rows = (
            step * state,
            step * (timed + state),
            back,
            back_timed,
            plain_sum,
            timed_sum,
            jnp.broadcast_to(skip_part, (SUBLANES, LANES)),
            zero,
        )
        for row, value in enumerate(rows):
            out_ref[pl.ds(base + row, SUBLANES, stride=ROWS_OUT), :] = value


def local_kernel(key_ref, value_ref, gate_ref, grad_ref, res_ref, rate_ref, skip_ref, fwd_ref, bwd_ref, before, after, taps):
    block, width = key_ref.shape
    modes = rate_ref.shape[0]
    groups = width // LANES
    chunks = block // SUBLANES
    zero = jnp.zeros((SUBLANES, LANES), jnp.float32)
    within = lax.broadcasted_iota(jnp.int32, (SUBLANES, LANES), 0).astype(jnp.float32)
    for group in range(groups):
        lanes = slice(group * LANES, (group + 1) * LANES)
        before[group, 0:SUBLANES, :] = zero
        before[group, SUBLANES:, :] = key_ref[:, lanes].astype(jnp.float32) * value_ref[:, lanes].astype(jnp.float32)
        after[group, 0:block, :] = grad_ref[:, lanes].astype(jnp.float32) * gate_ref[:, lanes].astype(jnp.float32)
        after[group, block:, :] = zero
        rate = jnp.exp(rate_ref[:, lanes])
        amplitude = res_ref[:, lanes] * jnp.sqrt(2.0 * rate / modes)
        stride = jnp.exp(-SUBLANES * rate)
        totals = [zero] * chunks
        for mode in range(modes):
            one = slice(mode, mode + 1)
            wave = jnp.broadcast_to(amplitude[one], (SUBLANES, LANES)) * jnp.exp(
                -jnp.broadcast_to(rate[one], (SUBLANES, LANES)) * within
            )
            jump = jnp.broadcast_to(stride[one], (SUBLANES, LANES))
            for chunk in range(chunks):
                totals[chunk] = totals[chunk] + wave
                if chunk + 1 < chunks:
                    wave = wave * jump
        for chunk in range(chunks):
            taps[group, chunk * SUBLANES : (chunk + 1) * SUBLANES, :] = totals[chunk]

    for group in range(groups):
        lanes = slice(group * LANES, (group + 1) * LANES)
        skip_row = jnp.broadcast_to(skip_ref[:, lanes], (SUBLANES, LANES))
        ahead = [skip_row * before[group, (c + 1) * SUBLANES : (c + 2) * SUBLANES, :] for c in range(chunks)]
        for shift in range(SUBLANES):
            moved = [before[group, pl.ds((c + 1) * SUBLANES - shift, SUBLANES), :] for c in range(chunks)]
            for lag in range(chunks):
                tap = jnp.broadcast_to(taps[group, pl.ds(lag * SUBLANES + shift, 1), :], (SUBLANES, LANES))
                for chunk in range(lag, chunks):
                    ahead[chunk] = ahead[chunk] + tap * moved[chunk - lag]
        for chunk in range(chunks):
            fwd_ref[chunk * SUBLANES : (chunk + 1) * SUBLANES, lanes] = ahead[chunk]
        back = [skip_row * after[group, c * SUBLANES : (c + 1) * SUBLANES, :] for c in range(chunks)]
        for shift in range(SUBLANES):
            moved = [after[group, pl.ds(c * SUBLANES + shift, SUBLANES), :] for c in range(chunks)]
            for lag in range(chunks):
                tap = jnp.broadcast_to(taps[group, pl.ds(lag * SUBLANES + shift, 1), :], (SUBLANES, LANES))
                for chunk in range(chunks - lag):
                    back[chunk] = back[chunk] + tap * moved[chunk + lag]
        for chunk in range(chunks):
            bwd_ref[chunk * SUBLANES : (chunk + 1) * SUBLANES, lanes] = back[chunk]


def shifted(value, amount):
    rows = lax.broadcasted_iota(jnp.int32, value.shape, 0)
    moved = pltpu.roll(value, amount % value.shape[0], 0)
    keep = rows >= amount if amount > 0 else rows < value.shape[0] + amount
    return jnp.where(keep, moved, 0.0)


def scan_kernel(block, modes, in_ref, res_ref, rate_ref, out_ref):
    chunk = SUBLANES
    rate = jnp.broadcast_to(jnp.exp(rate_ref[...]), (SUBLANES, LANES))
    unit = jnp.sqrt(2.0 * rate / modes)
    amplitude = jnp.broadcast_to(res_ref[...], (SUBLANES, LANES)) * unit
    power = [jnp.exp(-float(block * v) * rate) for v in range(chunk)]
    decay = power[1]

    def load(v, row):
        return in_ref[pl.ds(v * ROWS_OUT + row, SUBLANES, stride=chunk * ROWS_OUT), :]

    zero = jnp.zeros((SUBLANES, LANES), jnp.float32)
    state, timed, back = zero, zero, zero
    states, timeds, backs = [], [], [None] * chunk
    for v in range(chunk):
        states.append(state)
        timeds.append(timed)
        moved = decay * state
        timed = decay * timed + float(block) * moved + load(v, 1)
        state = moved + load(v, 0)
    for v in reversed(range(chunk)):
        backs[v] = back
        back = decay * back + load(v, 2)
    span = block * chunk
    distance = 1
    while distance < SUBLANES:
        far = jnp.exp(-float(span * distance) * rate)
        older = far * shifted(state, distance)
        timed = timed + far * shifted(timed, distance) + float(span * distance) * older
        state = state + older
        back = back + far * shifted(back, -distance)
        distance *= 2
    state, timed, back = shifted(state, 1), shifted(timed, 1), shifted(back, -1)
    plain, slow, skip = zero, zero, zero
    for v in range(chunk):
        entering = states[v] + power[v] * state
        entering_timed = timeds[v] + power[v] * (timed + float(block * v) * state)
        leaving = backs[v] + power[chunk - 1 - v] * back
        slope, slope_timed = load(v, 2), load(v, 3)
        plain = plain + load(v, 4) + slope * entering
        slow = slow + load(v, 5) + slope_timed * entering + slope * entering_timed
        skip = skip + load(v, 6)
        out_ref[pl.ds(v * ROWS_BACK, SUBLANES, stride=chunk * ROWS_BACK), :] = entering
        out_ref[pl.ds(v * ROWS_BACK + 1, SUBLANES, stride=chunk * ROWS_BACK), :] = leaving

    def total(value):
        return jnp.broadcast_to(jnp.sum(value, axis=0, keepdims=True), (SUBLANES, LANES))

    plain, slow, skip = total(plain), total(slow), total(skip)
    raw_res = plain * unit
    raw_log = (0.5 * plain - rate * slow) * amplitude
    for v in range(chunk):
        for row, value in ((2, raw_res), (3, raw_log), (4, skip)):
            out_ref[pl.ds(v * ROWS_BACK + row, SUBLANES, stride=chunk * ROWS_BACK), :] = value


def square_kernel(modes, in_ref, res_ref, log_ref, skip_ref, out_ref):
    groups = res_ref.shape[1] // LANES
    total = jnp.zeros((SUBLANES, LANES), jnp.float32)
    for group in range(groups):
        lanes = slice(group * LANES, (group + 1) * LANES)
        for half in range(modes // SUBLANES):
            base = (group * modes + half * SUBLANES) * ROWS_BACK
            rows = slice(half * SUBLANES, (half + 1) * SUBLANES)
            for row, ref in ((2, res_ref), (3, log_ref)):
                value = in_ref[pl.ds(base + row, SUBLANES, stride=ROWS_BACK), :]
                ref[rows, lanes] = value
                total = total + value * value
        skip = in_ref[pl.ds(group * modes * ROWS_BACK + 4, 1), :]
        skip_ref[:, lanes] = skip
        first = lax.broadcasted_iota(jnp.int32, (SUBLANES, LANES), 0) == 0
        total = total + jnp.where(first, skip * skip, 0.0)
    out_ref[...] = jnp.broadcast_to(jnp.sum(total, axis=0, keepdims=True)[None], out_ref.shape)


def clip_kernel(count, squares_ref, res_ref, log_ref, skip_ref, out_res, out_log, out_skip):
    squares = jnp.sum(jnp.sum(squares_ref[...], axis=0), axis=1, keepdims=True)
    factor = CLIP_RMS / jnp.maximum(jnp.sqrt(squares / count), CLIP_RMS)
    out_res[...] = res_ref[...] * factor
    out_log[...] = log_ref[...] * factor
    out_skip[...] = skip_ref[...] * factor


def output_kernel(in_ref, fwd_ref, bwd_ref, key_ref, value_ref, gate_ref, grad_ref, res_ref, rate_ref, out_ref, gate_out, key_out, value_out):
    block, width = key_ref.shape
    modes = rate_ref.shape[0]
    groups = width // LANES
    chunks = block // SUBLANES
    within = lax.broadcasted_iota(jnp.int32, (SUBLANES, LANES), 0).astype(jnp.float32)
    for group in range(groups):
        lanes = slice(group * LANES, (group + 1) * LANES)
        rate = jnp.exp(rate_ref[:, lanes])
        amplitude = res_ref[:, lanes] * jnp.sqrt(2.0 * rate / modes)
        stride = jnp.exp(-SUBLANES * rate)
        ahead = [fwd_ref[c * SUBLANES : (c + 1) * SUBLANES, lanes] for c in range(chunks)]
        back = [bwd_ref[c * SUBLANES : (c + 1) * SUBLANES, lanes] for c in range(chunks)]
        for mode in range(modes):
            one = slice(mode, mode + 1)
            base = (group * modes + mode) * ROWS_BACK
            rate_row = jnp.broadcast_to(rate[one], (SUBLANES, LANES))
            jump = jnp.broadcast_to(stride[one], (SUBLANES, LANES))
            wave = jnp.broadcast_to(amplitude[one] * in_ref[pl.ds(base, 1), :], (SUBLANES, LANES)) * jnp.exp(-rate_row * within)
            echo = jnp.broadcast_to(amplitude[one] * in_ref[pl.ds(base + 1, 1), :], (SUBLANES, LANES)) * jnp.exp(
                -rate_row * (float(SUBLANES) - within)
            )
            for chunk in range(chunks):
                ahead[chunk] = ahead[chunk] + wave
                back[chunks - 1 - chunk] = back[chunks - 1 - chunk] + echo
                if chunk + 1 < chunks:
                    wave = wave * jump
                    echo = echo * jump
        for pair in range(chunks // 2):
            rows = slice(pair * 2 * SUBLANES, (pair + 1) * 2 * SUBLANES)
            filtered = jnp.concatenate([ahead[2 * pair], ahead[2 * pair + 1]], axis=0)
            mixed_grad = jnp.concatenate([back[2 * pair], back[2 * pair + 1]], axis=0)
            out_ref[rows, lanes] = (gate_ref[rows, lanes].astype(jnp.float32) * filtered).astype(jnp.bfloat16)
            gate_out[rows, lanes] = (grad_ref[rows, lanes].astype(jnp.float32) * filtered).astype(jnp.bfloat16)
            key_out[rows, lanes] = (value_ref[rows, lanes].astype(jnp.float32) * mixed_grad).astype(jnp.bfloat16)
            value_out[rows, lanes] = (key_ref[rows, lanes].astype(jnp.float32) * mixed_grad).astype(jnp.bfloat16)


def call(kernel, out_shape, *args, scratch=()):
    multiple = isinstance(out_shape, (tuple, list))
    return pl.pallas_call(
        kernel,
        out_shape=out_shape,
        in_specs=[VMEM] * len(args),
        out_specs=[VMEM] * len(out_shape) if multiple else VMEM,
        scratch_shapes=list(scratch),
        compiler_params=PARAMS,
    )(*args)


def floats(*shape):
    return jax.ShapeDtypeStruct(shape, jnp.float32)


def per_device(gate_in, key_in, value_in, out_grad, residue, log_rate, skip):
    block, width = gate_in.shape
    modes = residue.shape[0]
    blocks = lax.axis_size("seq")
    shards = lax.axis_size("chan")
    groups = width // LANES
    owners = groups * modes
    assert owners == blocks
    device = lax.axis_index("seq")
    own_mode, own_group = device % modes, device // modes
    own_rate = lax.dynamic_slice(log_rate, (own_mode, own_group * LANES), (1, LANES))
    own_res = lax.dynamic_slice(residue, (own_mode, own_group * LANES), (1, LANES))
    skip_row = skip.reshape(1, width)

    sent = call(
        summary_kernel,
        floats(owners * ROWS_OUT, LANES),
        key_in, value_in, gate_in, out_grad, log_rate,
        scratch=[pltpu.VMEM((block, width), jnp.float32)] * 2,
    )
    arrived = lax.all_to_all(sent.reshape(owners, ROWS_OUT, LANES), "seq", 0, 0, tiled=True)
    forward, backward = call(
        local_kernel,
        (floats(block, width), floats(block, width)),
        key_in, value_in, gate_in, out_grad, residue, log_rate, skip_row,
        scratch=[
            pltpu.VMEM((groups, block + SUBLANES, LANES), jnp.float32),
            pltpu.VMEM((groups, block + SUBLANES, LANES), jnp.float32),
            pltpu.VMEM((groups, block, LANES), jnp.float32),
        ],
    )
    reply = call(
        functools.partial(scan_kernel, block, modes),
        floats(blocks * ROWS_BACK, LANES),
        arrived.reshape(blocks * ROWS_OUT, LANES), own_res, own_rate,
    )
    states = lax.all_to_all(reply.reshape(blocks, ROWS_BACK, LANES), "seq", 0, 0, tiled=True)
    states = states.reshape(owners * ROWS_BACK, LANES)
    raw_res, raw_log, raw_skip, squares = call(
        functools.partial(square_kernel, modes),
        (floats(modes, width), floats(modes, width), floats(1, width), floats(shards, 1, LANES)),
        states,
    )
    squares = lax.all_to_all(squares, "chan", 0, 0, tiled=True)
    gated_out, gate_grad, key_grad, value_grad = call(
        output_kernel,
        (jax.ShapeDtypeStruct((block, width), jnp.bfloat16),) * 4,
        states, forward, backward, key_in, value_in, gate_in, out_grad, residue, log_rate,
    )
    residue_grad, log_rate_grad, skip_grad = call(
        functools.partial(clip_kernel, float((2 * modes + 1) * width * shards)),
        (floats(modes, width), floats(modes, width), floats(1, width)),
        squares, raw_res, raw_log, raw_skip,
    )
    return gated_out, gate_grad, key_grad, value_grad, residue_grad, log_rate_grad, skip_grad.reshape(width)


def solution(mesh):
    field, parameter, gain = P("seq", "chan"), P(None, "chan"), P("chan")
    return jax.shard_map(
        per_device,
        mesh=mesh,
        in_specs=(field, field, field, field, parameter, parameter, gain),
        out_specs=(field, field, field, field, parameter, parameter, gain),
        check_vma=False,
    )
```

time: 892 us -> 70.7 us (0.08)
  the two profiles are of different devices: /device:TPU:2 before, /device:TPU:8 now
where the time goes in v1:
time: 70.7 us; the launch traced here: 70.2 us
  starting transfers between devices  21.4 us (30%)
  blocking collectives  17.6 us (25%)
  waiting for transfers between devices  16.7 us (24%)
  Pallas kernels  8.56 us (12%)
  local copies, waits for them, and re-layouts  5.27 us (7%)
  between operations  0.76 us (1%)
    all_to_all x1, blocking collectives, per_device(): lax.all_to_all(reply.reshape(blocks, ROWS_BACK, LANES), 'seq', 0, 0, tile...  17.6 us
    all_to_all x1, starting transfers between devices, per_device(): lax.all_to_all(sent.reshape(owners, ROWS_OUT, LANES), 'seq', 0, 0, tiled=...  14.5 us
    all_to_all x1, waiting for transfers between devices, per_device(): lax.all_to_all(sent.reshape(owners, ROWS_OUT, LANES), 'seq', 0, 0, tiled=...  11 us
    pallas_call x6, Pallas kernels, call(): pl.pallas_call(kernel, out_shape=out_shape, in_specs=[VMEM] * len(args),...  8.56 us
    all_to_all x1, starting transfers between devices, per_device(): squares = lax.all_to_all(squares, 'chan', 0, 0, tiled=True)  6.86 us
    all_to_all x1, waiting for transfers between devices, per_device(): squares = lax.all_to_all(squares, 'chan', 0, 0, tiled=True)  5.64 us
    unnamed x24, local copies, waits for them, and re-layouts  5.12 us
  transfers between devices with their start and end apart: 2, of which 2 were waited for; matrix products, arithmetic and copies ran while one was open for 0% of the time, Pallas kernels for 6%

profile of v1, /device:TPU:8, one launch (start us, length us, event | category | flops | bytes accessed | tf_op | source)
XLA Modules:
  0.0 70.2 jit_solution(5431196671563429891)
XLA Ops:
  0.6 0.0 copy-start
  0.6 0.9 %copy-done = bf16[128,512]{1,0:T(8,128)(2,1)S(1)} copy-done((bf16[128,512]{1,0:T(8,128)(2,1)S(1)}, bf16[128,512]{1,0:T(8,128)(2,1)}, u32[]{:S(2)}) %copy-start) | copy-done | bytes 131096
  1.5 0.0 copy-start.2
  1.5 0.9 %copy-done.2 = bf16[128,512]{1,0:T(8,128)(2,1)S(1)} copy-done((bf16[128,512]{1,0:T(8,128)(2,1)S(1)}, bf16[128,512]{1,0:T(8,128)(2,1)}, u32[]{:S(2)}) %copy-start.2) | copy-done | bytes 131096
  2.4 0.0 copy-start.4
  2.4 0.9 %copy-done.4 = bf16[128,512]{1,0:T(8,128)(2,1)S(1)} copy-done((bf16[128,512]{1,0:T(8,128)(2,1)S(1)}, bf16[128,512]{1,0:T(8,128)(2,1)}, u32[]{:S(2)}) %copy-start.4) | copy-done | bytes 131096
  3.3 0.0 copy-start.6
  3.4 0.9 %copy-done.6 = bf16[128,512]{1,0:T(8,128)(2,1)S(1)} copy-done((bf16[128,512]{1,0:T(8,128)(2,1)S(1)}, bf16[128,512]{1,0:T(8,128)(2,1)}, u32[]{:S(2)}) %copy-start.6) | copy-done | bytes 131096
  4.3 0.8 %copy-done.8 = f32[16,512]{1,0:T(8,128)S(1)} copy-done((f32[16,512]{1,0:T(8,128)S(1)}, f32[16,512]{1,0:T(8,128)}, u32[]{:S(2)}) %copy-start.8) | copy-done | bytes 32792
  5.0 2.7 %shard_map.126 = f32[512,128]{1,0:T(8,128)} custom-call(bf16[128,512]{1,0:T(8,128)(2,1)S(1)} %copy-done, bf16[128,512]{1,0:T(8,128)(2,1)S(1)} %copy-done.2, bf16[128,512]{1,0:T(8,128)(2,1)S(1)} %copy-done.4, bf16[128,512]{1,0:T(8,128)(2,1)S(1)} %copy-done.6, f32[16,512]{1,0:T(8,128)S(1)} %copy-done.8), custom_call_target="tpu_custom_call" | custom-call | tf_op jit(solution)/shard_map/pallas_call | solution.py:268
  7.7 14.5 %all-to-all-start = ((f32[64,8,128]{2,1,0:T(8,128)}), f32[64,8,128]{2,1,0:T(8,128)S(1)}, u32[]{:S(2)}, u32[]{:S(2)}) async-start(f32[64,8,128]{2,1,0:T(8,128)} %bitcast), calls=%async_computation | async-start | bytes 524288 | tf_op jit(solution)/shard_map/all_to_all | solution.py:302
  22.2 0.0 copy-start.9
  22.2 0.7 %copy-done.9 = f32[16,512]{1,0:T(8,128)S(1)} copy-done((f32[16,512]{1,0:T(8,128)S(1)}, f32[16,512]{1,0:T(8,128)}, u32[]{:S(2)}) %copy-start.9) | copy-done | bytes 32792
  23.0 0.1 dynamic_slice.7.rate_ref
  23.0 0.0 copy-done.10
  23.0 0.1 dynamic_slice.6.res_ref
  23.1 11.0 %all-to-all-done = f32[64,8,128]{2,1,0:T(8,128)S(1)} async-done(((f32[64,8,128]{2,1,0:T(8,128)}), f32[64,8,128]{2,1,0:T(8,128)S(1)}, u32[]{:S(2)}, u32[]{:S(2)}) %all-to-all-start) | async-done | bytes 262176 | tf_op jit(solution)/shard_map/all_to_all | solution.py:302
  34.2 0.2 shard_map.127
  34.4 0.0 copy-start.5
  34.4 0.0 copy-start.7
  34.4 17.6 %all_to_all.15 = f32[64,8,128]{2,1,0:T(8,128)S(1)} all-to-all(f32[64,8,128]{2,1,0:T(8,128)S(1)} %bitcast.9), channel_id=1, replica_groups=mesh['seq'=64,'chan'=8] {'seq'}, dimensions={0} | all-to-all | bytes 524288 | tf_op jit(solution)/shard_map/all_to_all | solution.py:318
  52.0 0.6 shard_map.130
  52.6 6.9 %all-to-all-start.2 = ((f32[8,1,128]{2,1,0:T(1,128)}), f32[8,1,128]{2,1,0:T(1,128)S(1)}, u32[]{:S(2)}, u32[]{:S(2)}) async-start(f32[8,1,128]{2,1,0:T(1,128)} %get-tuple-element.26), calls=%async_computation.2 | async-start | bytes 8192 | tf_op jit(solution)/shard_map/all_to_all | solution.py:325
  59.5 0.0 copy-done.5
  59.5 0.0 copy-done.7
  59.5 0.0 copy-done.1
  59.5 0.0 copy-done.3
  59.5 0.0 copy-done.11
  59.5 2.7 %shard_map.128 = (f32[128,512]{1,0:T(8,128)S(1)}, f32[128,512]{1,0:T(8,128)S(1)}) custom-call(bf16[128,512]{1,0:T(8,128)(2,1)S(1)} %copy-done.1, bf16[128,512]{1,0:T(8,128)(2,1)S(1)} %copy-done.3, bf16[128,512]{1,0:T(8,128)(2,1)S(1)} %copy-done.5, bf16[128,512]{1,0:T(8,128)(2,1)S(1)} %copy-done.7, f32[16,512]{1,0:T(8,128)S(1)} %copy-done.10, ...), custom_call_target="tpu_custom_call" | custom-call | tf_op jit(solution)/shard_map/pallas_call | solution.py:268
  62.3 1.6 %shard_map.129 = (bf16[128,512]{1,0:T(8,128)(2,1)}, bf16[128,512]{1,0:T(8,128)(2,1)}, bf16[128,512]{1,0:T(8,128)(2,1)}, bf16[128,512]{1,0:T(8,128)(2,1)}) custom-call(f32[512,128]{1,0:T(8,128)S(1)} %bitcast.7, f32[128,512]{1,0:T(8,128)S(1)} %get-tuple-element.20.fwd_ref, f32[128,512]{1,0:T(8,128)S(1)} %get-tuple-element.21.bwd_ref, ...), custom_call_target="tpu_custom_call" | custom-call | tf_op jit(solution)/shard_map/pallas_call | solution.py:268
  63.8 5.6 %all-to-all-done.2.squares_ref = f32[8,1,128]{2,1,0:T(1,128)S(1)} async-done(((f32[8,1,128]{2,1,0:T(1,128)}), f32[8,1,128]{2,1,0:T(1,128)S(1)}, u32[]{:S(2)}, u32[]{:S(2)}) %all-to-all-start.2) | async-done | bytes 4128 | tf_op jit(solution)/shard_map/all_to_all | solution.py:325
  69.5 0.7 %shard_map.131 = (f32[16,512]{1,0:T(8,128)}, f32[16,512]{1,0:T(8,128)}, f32[1,512]{1,0:T(1,128)}) custom-call(f32[8,1,128]{2,1,0:T(1,128)S(1)} %all-to-all-done.2.squares_ref, f32[16,512]{1,0:T(8,128)S(1)} %get-tuple-element.27.res_ref, f32[16,512]{1,0:T(8,128)S(1)} %get-tuple-element.28.log_ref, f32[1,512]{1,0:T(1,128)S(1)} %get-tuple-element.29.skip_ref), custom_call_target="tpu_custom_call" | custom-call | tf_op jit(solution)/shard_map/pallas_call | solution.py:268
  (5 shorter events, 0.0 us)
Async XLA Ops:
  0.6 0.9 %copy-start = (bf16[128,512]{1,0:T(8,128)(2,1)S(1)}, bf16[128,512]{1,0:T(8,128)(2,1)}, u32[]{:S(2)}) copy-start(bf16[128,512]{1,0:T(8,128)(2,1)} %key_ref.5) | copy-start | bytes 393220
  1.5 0.9 %copy-start.2 = (bf16[128,512]{1,0:T(8,128)(2,1)S(1)}, bf16[128,512]{1,0:T(8,128)(2,1)}, u32[]{:S(2)}) copy-start(bf16[128,512]{1,0:T(8,128)(2,1)} %value_ref.5) | copy-start | bytes 393220
  2.4 0.9 %copy-start.4 = (bf16[128,512]{1,0:T(8,128)(2,1)S(1)}, bf16[128,512]{1,0:T(8,128)(2,1)}, u32[]{:S(2)}) copy-start(bf16[128,512]{1,0:T(8,128)(2,1)} %gate_ref.5) | copy-start | bytes 393220
  3.3 0.9 %copy-start.6 = (bf16[128,512]{1,0:T(8,128)(2,1)S(1)}, bf16[128,512]{1,0:T(8,128)(2,1)}, u32[]{:S(2)}) copy-start(bf16[128,512]{1,0:T(8,128)(2,1)} %grad_ref.5) | copy-start | bytes 393220
  4.3 0.8 %copy-start.8 = (f32[16,512]{1,0:T(8,128)S(1)}, f32[16,512]{1,0:T(8,128)}, u32[]{:S(2)}) copy-start(f32[16,512]{1,0:T(8,128)} %rate_ref.5) | copy-start | bytes 98308
  7.7 15.3 %copy-start.10 = (f32[16,512]{1,0:T(8,128)S(1)}, f32[16,512]{1,0:T(8,128)}, u32[]{:S(2)}) copy-start(f32[16,512]{1,0:T(8,128)} %res_ref.3) | copy-start | bytes 98308
  7.7 26.5 %all-to-all-start = ((f32[64,8,128]{2,1,0:T(8,128)}), f32[64,8,128]{2,1,0:T(8,128)S(1)}, u32[]{:S(2)}, u32[]{:S(2)}) async-start(f32[64,8,128]{2,1,0:T(8,128)} %bitcast), calls=%async_computation | async-start | bytes 524288 | tf_op jit(solution)/shard_map/all_to_all | solution.py:302
  22.2 0.8 %copy-start.9 = (f32[16,512]{1,0:T(8,128)S(1)}, f32[16,512]{1,0:T(8,128)}, u32[]{:S(2)}) copy-start(f32[16,512]{1,0:T(8,128)} %rate_ref.5) | copy-start | bytes 98308
  34.4 25.1 %copy-start.5 = (bf16[128,512]{1,0:T(8,128)(2,1)S(1)}, bf16[128,512]{1,0:T(8,128)(2,1)}, u32[]{:S(2)}) copy-start(bf16[128,512]{1,0:T(8,128)(2,1)} %gate_ref.5) | copy-start | bytes 393220
  34.4 25.1 %copy-start.7 = (bf16[128,512]{1,0:T(8,128)(2,1)S(1)}, bf16[128,512]{1,0:T(8,128)(2,1)}, u32[]{:S(2)}) copy-start(bf16[128,512]{1,0:T(8,128)(2,1)} %grad_ref.5) | copy-start | bytes 393220
  52.0 7.5 %copy-start.1 = (bf16[128,512]{1,0:T(8,128)(2,1)S(1)}, bf16[128,512]{1,0:T(8,128)(2,1)}, u32[]{:S(2)}) copy-start(bf16[128,512]{1,0:T(8,128)(2,1)} %key_ref.5) | copy-start | bytes 393220
  52.0 7.5 %copy-start.3 = (bf16[128,512]{1,0:T(8,128)(2,1)S(1)}, bf16[128,512]{1,0:T(8,128)(2,1)}, u32[]{:S(2)}) copy-start(bf16[128,512]{1,0:T(8,128)(2,1)} %value_ref.5) | copy-start | bytes 393220
  52.0 7.5 %copy-start.11 = (f32[512]{0:T(512)S(1)}, f32[512]{0:T(512)}, u32[]{:S(2)}) copy-start(f32[512]{0:T(512)} %param.13) | copy-start | bytes 6148
  52.6 16.8 %all-to-all-start.2 = ((f32[8,1,128]{2,1,0:T(1,128)}), f32[8,1,128]{2,1,0:T(1,128)S(1)}, u32[]{:S(2)}, u32[]{:S(2)}) async-start(f32[8,1,128]{2,1,0:T(1,128)} %get-tuple-element.26), calls=%async_computation.2 | async-start | bytes 8192 | tf_op jit(solution)/shard_map/all_to_all | solution.py:325

commit v2 on v1

--- a/solution.py
+++ b/solution.py
@@ -10,8 +10,9 @@
 CLIP_RMS = 1.0
 LANES = 128
 SUBLANES = 8
-ROWS_OUT = 8
-ROWS_BACK = 8
+ROWS_OUT = 7
+ROWS_BACK = 5
+Y_RUN = 4
 VMEM = pl.BlockSpec(memory_space=pltpu.VMEM)
 PARAMS = pltpu.CompilerParams(vmem_limit_bytes=32 * 1024 * 1024)
 
@@ -24,17 +25,26 @@
     return jnp.broadcast_to(tile[row : row + 1], (SUBLANES, LANES))
 
 
-def summary_kernel(key_ref, value_ref, gate_ref, grad_ref, rate_ref, out_ref, mixed, slope):
+def summary_kernel(key_hbm, value_hbm, gate_hbm, grad_hbm, rate_hbm, out_ref, key_ref, value_ref, gate_ref, grad_ref, rate_ref, mixed, slope, sems):
     block, width = key_ref.shape
     modes = rate_ref.shape[0]
     halves, groups = modes // SUBLANES, width // LANES
-    mixed[...] = key_ref[...].astype(jnp.float32) * value_ref[...].astype(jnp.float32)
-    slope[...] = grad_ref[...].astype(jnp.float32) * gate_ref[...].astype(jnp.float32)
+    pairs = ((rate_hbm, rate_ref), (key_hbm, key_ref), (value_hbm, value_ref), (grad_hbm, grad_ref), (gate_hbm, gate_ref))
+    copies = [pltpu.make_async_copy(source, target, sems.at[at]) for at, (source, target) in enumerate(pairs)]
+    for copy in copies:
+        copy.start()
+    copies[0].wait()
     steps = {}
     for half in range(halves):
         for group in range(groups):
             rate = jnp.exp(rate_ref[half * SUBLANES : (half + 1) * SUBLANES, group * LANES : (group + 1) * LANES])
             steps[half, group] = jnp.exp(-rate)
+    copies[1].wait()
+    copies[2].wait()
+    mixed[...] = key_ref[...].astype(jnp.float32) * value_ref[...].astype(jnp.float32)
+    copies[3].wait()
+    copies[4].wait()
+    slope[...] = grad_ref[...].astype(jnp.float32) * gate_ref[...].astype(jnp.float32)
     zero = jnp.zeros((SUBLANES, LANES), jnp.float32)
     keys = [(half, group) for half in range(halves) for group in range(groups)]
 
@@ -76,7 +86,6 @@
             plain_sum,
             timed_sum,
             jnp.broadcast_to(skip_part, (SUBLANES, LANES)),
-            zero,
         )
         for row, value in enumerate(rows):
             out_ref[pl.ds(base + row, SUBLANES, stride=ROWS_OUT), :] = value
@@ -214,11 +223,11 @@
         skip_ref[:, lanes] = skip
         first = lax.broadcasted_iota(jnp.int32, (SUBLANES, LANES), 0) == 0
         total = total + jnp.where(first, skip * skip, 0.0)
-    out_ref[...] = jnp.broadcast_to(jnp.sum(total, axis=0, keepdims=True)[None], out_ref.shape)
+    out_ref[...] = jnp.broadcast_to(jnp.sum(total, axis=0, keepdims=True), out_ref.shape)
 
 
 def clip_kernel(count, squares_ref, res_ref, log_ref, skip_ref, out_res, out_log, out_skip):
-    squares = jnp.sum(jnp.sum(squares_ref[...], axis=0), axis=1, keepdims=True)
+    squares = jnp.sum(jnp.sum(squares_ref[...], axis=0, keepdims=True), axis=1, keepdims=True)
     factor = CLIP_RMS / jnp.maximum(jnp.sqrt(squares / count), CLIP_RMS)
     out_res[...] = res_ref[...] * factor
     out_log[...] = log_ref[...] * factor
@@ -263,16 +272,35 @@
             value_out[rows, lanes] = (key_ref[rows, lanes].astype(jnp.float32) * mixed_grad).astype(jnp.bfloat16)
 
 
-def call(kernel, out_shape, *args, scratch=()):
+def in_hbm(*arrays):
+    return tuple(pltpu.with_memory_space_constraint(array, pltpu.HBM) for array in arrays)
+
+
+def call(kernel, out_shape, *args, scratch=(), space=VMEM):
     multiple = isinstance(out_shape, (tuple, list))
     return pl.pallas_call(
         kernel,
         out_shape=out_shape,
-        in_specs=[VMEM] * len(args),
+        in_specs=[space] * len(args),
         out_specs=[VMEM] * len(out_shape) if multiple else VMEM,
         scratch_shapes=list(scratch),
         compiler_params=PARAMS,
     )(*args)
+
+
+def exchange(rows, axis, groups=None):
+    count, lanes = rows.shape
+    moved = lax.all_to_all(rows.reshape(count, 1, lanes), axis, 0, 0, axis_index_groups=groups, tiled=True)
+    return moved.reshape(count, lanes)
+
+
+def near_groups(blocks, shards):
+    run = blocks // Y_RUN
+    groups = []
+    for device in range(blocks):
+        other = device ^ (2 * run)
+        groups.append([(other if shard % 2 else device) * shards + shard for shard in range(shards)])
+    return groups
 
 
 def floats(*shape):
@@ -296,10 +324,14 @@
     sent = call(
         summary_kernel,
         floats(owners * ROWS_OUT, LANES),
-        key_in, value_in, gate_in, out_grad, log_rate,
-        scratch=[pltpu.VMEM((block, width), jnp.float32)] * 2,
-    )
-    arrived = lax.all_to_all(sent.reshape(owners, ROWS_OUT, LANES), "seq", 0, 0, tiled=True)
+        *in_hbm(key_in, value_in, gate_in, out_grad, log_rate),
+        scratch=[pltpu.VMEM((block, width), jnp.bfloat16)] * 4
+        + [pltpu.VMEM((modes, width), jnp.float32)]
+        + [pltpu.VMEM((block, width), jnp.float32)] * 2
+        + [pltpu.SemaphoreType.DMA((5,))],
+        space=pl.BlockSpec(memory_space=pltpu.HBM),
+    )
+    arrived = exchange(sent, "seq")
     forward, backward = call(
         local_kernel,
         (floats(block, width), floats(block, width)),
@@ -310,19 +342,19 @@
             pltpu.VMEM((groups, block, LANES), jnp.float32),
         ],
     )
+    arrived, forward, backward = lax.optimization_barrier((arrived, forward, backward))
     reply = call(
         functools.partial(scan_kernel, block, modes),
         floats(blocks * ROWS_BACK, LANES),
-        arrived.reshape(blocks * ROWS_OUT, LANES), own_res, own_rate,
-    )
-    states = lax.all_to_all(reply.reshape(blocks, ROWS_BACK, LANES), "seq", 0, 0, tiled=True)
-    states = states.reshape(owners * ROWS_BACK, LANES)
+        arrived, own_res, own_rate,
+    )
+    states = exchange(reply, "seq")
     raw_res, raw_log, raw_skip, squares = call(
         functools.partial(square_kernel, modes),
-        (floats(modes, width), floats(modes, width), floats(1, width), floats(shards, 1, LANES)),
+        (floats(modes, width), floats(modes, width), floats(1, width), floats(shards, LANES)),
         states,
     )
-    squares = lax.all_to_all(squares, "chan", 0, 0, tiled=True)
+    squares = exchange(squares, ("seq", "chan"), near_groups(blocks, shards))
     gated_out, gate_grad, key_grad, value_grad = call(
         output_kernel,
         (jax.ShapeDtypeStruct((block, width), jnp.bfloat16),) * 4,

time: 70.7 us -> 62.3 us (0.88)
  local copies, waits for them, and re-layouts: 5.27 us -> 0.19 us
  blocking collectives: 17.6 us -> 15.1 us
  waiting for transfers between devices: 16.7 us -> 15 us
  Pallas kernels: 8.56 us -> 9.53 us
    unnamed x24 -> x14, local copies, waits for them, and re-layouts: 5.12 us -> 0.04 us
    all_to_all x1, blocking collectives: 17.6 us -> 15.1 us  [exchange(): lax.all_to_all(rows.reshape(count, 1, lanes), axis, 0, 0, axis_index_grou...]
    all_to_all x2, waiting for transfers between devices: 16.7 us -> 15 us  [exchange(): lax.all_to_all(rows.reshape(count, 1, lanes), axis, 0, 0, axis_index_grou...]
    pallas_call x6, Pallas kernels: 8.56 us -> 9.53 us  [call(): pl.pallas_call(kernel, out_shape=out_shape, in_specs=[space] * len(args),...]
  transfers between devices with their start and end apart: 2 -> 2, of which waited for: 2 -> 2; matrix products, arithmetic and copies ran while one was open for 0% -> 0% of each run, Pallas kernels for 6% -> 7%
where the time goes in v2:
time: 62.3 us; the launch traced here: 62 us
  starting transfers between devices  21.4 us (34%)
  blocking collectives  15.1 us (24%)
  waiting for transfers between devices  15 us (24%)
  Pallas kernels  9.53 us (15%)
  between operations  0.77 us (1%)
    all_to_all x2, starting transfers between devices, exchange(): lax.all_to_all(rows.reshape(count, 1, lanes), axis, 0, 0, axis_index_grou...  21.4 us
    all_to_all x1, blocking collectives, exchange(): lax.all_to_all(rows.reshape(count, 1, lanes), axis, 0, 0, axis_index_grou...  15.1 us
    all_to_all x2, waiting for transfers between devices, exchange(): lax.all_to_all(rows.reshape(count, 1, lanes), axis, 0, 0, axis_index_grou...  15 us
    pallas_call x6, Pallas kernels, call(): pl.pallas_call(kernel, out_shape=out_shape, in_specs=[space] * len(args),...  9.53 us
  transfers between devices with their start and end apart: 2, of which 2 were waited for; matrix products, arithmetic and copies ran while one was open for 0% of the time, Pallas kernels for 7%

profile of v2, /device:TPU:8, one launch (start us, length us, event | category | flops | bytes accessed | tf_op | source)
XLA Modules:
  0.0 62.0 jit_solution(4885065652452803430)
XLA Ops:
  0.6 0.0 copy-start.4
  0.6 0.0 copy-start.5
  0.7 0.0 copy-start.6
  0.7 3.8 %shard_map.126 = f32[448,128]{1,0:T(8,128)} custom-call(bf16[128,512]{1,0:T(8,128)(2,1)} %key_ref.3, bf16[128,512]{1,0:T(8,128)(2,1)} %value_ref.3, bf16[128,512]{1,0:T(8,128)(2,1)} %gate_ref.3, bf16[128,512]{1,0:T(8,128)(2,1)} %grad_ref.3, f32[16,512]{1,0:T(8,128)} %rate_ref.3), custom_call_target="tpu_custom_call" | custom-call | tf_op jit(solution)/shard_map/pallas_call | solution.py:281
  4.5 0.0 copy-start.3
  4.5 0.0 copy-start
  4.5 0.0 copy-start.1
  4.5 0.0 copy-start.2
  4.5 14.5 %all-to-all-start = ((f32[448,1,128]{2,1,0:T(1,128)}), f32[448,1,128]{2,1,0:T(1,128)S(1)}, u32[]{:S(2)}, u32[]{:S(2)}) async-start(f32[448,1,128]{2,1,0:T(1,128)} %bitcast.1), calls=%async_computation | async-start | bytes 458752 | tf_op jit(solution)/shard_map/all_to_all | solution.py:293
  19.1 0.0 copy-done.4
  19.1 0.1 dynamic_slice.7.rate_ref
  19.1 0.0 copy-done.5
  19.1 0.1 dynamic_slice.6.res_ref
  19.2 0.0 copy-done.6
  19.2 0.0 copy-done.3
  19.2 0.0 copy-done
  19.2 0.0 copy-done.1
  19.2 0.0 copy-done.2
  19.2 2.7 %shard_map.127 = (f32[128,512]{1,0:T(8,128)S(1)}, f32[128,512]{1,0:T(8,128)S(1)}) custom-call(bf16[128,512]{1,0:T(8,128)(2,1)S(1)} %copy-done, bf16[128,512]{1,0:T(8,128)(2,1)S(1)} %copy-done.1, bf16[128,512]{1,0:T(8,128)(2,1)S(1)} %copy-done.2, bf16[128,512]{1,0:T(8,128)(2,1)S(1)} %copy-done.3, f32[16,512]{1,0:T(8,128)S(1)} %copy-done.5, ...), custom_call_target="tpu_custom_call" | custom-call | tf_op jit(solution)/shard_map/pallas_call | solution.py:281
  22.0 8.4 %all-to-all-done = f32[448,1,128]{2,1,0:T(1,128)S(1)} async-done(((f32[448,1,128]{2,1,0:T(1,128)}), f32[448,1,128]{2,1,0:T(1,128)S(1)}, u32[]{:S(2)}, u32[]{:S(2)}) %all-to-all-start) | async-done | bytes 229408 | tf_op jit(solution)/shard_map/all_to_all | solution.py:293
  30.3 0.1 shard_map.128
  30.4 15.1 %all_to_all.15 = f32[320,1,128]{2,1,0:T(1,128)S(1)} all-to-all(f32[320,1,128]{2,1,0:T(1,128)S(1)} %bitcast.17), channel_id=1, replica_groups=mesh['seq'=64,'chan'=8] {'seq'}, dimensions={0} | all-to-all | bytes 327680 | tf_op jit(solution)/shard_map/all_to_all | solution.py:293
  45.6 0.6 %shard_map.130 = (f32[16,512]{1,0:T(8,128)S(1)}, f32[16,512]{1,0:T(8,128)S(1)}, f32[1,512]{1,0:T(1,128)S(1)}, f32[8,128]{1,0:T(8,128)}) custom-call(f32[320,128]{1,0:T(8,128)S(1)} %bitcast.14), custom_call_target="tpu_custom_call" | custom-call | tf_op jit(solution)/shard_map/pallas_call | solution.py:281
  46.2 6.9 %all-to-all-start.2 = ((f32[8,1,128]{2,1,0:T(1,128)}), f32[8,1,128]{2,1,0:T(1,128)S(1)}, u32[]{:S(2)}, u32[]{:S(2)}) async-start(f32[8,1,128]{2,1,0:T(1,128)} %bitcast.8), calls=%async_computation.2 | async-start | bytes 8192 | tf_op jit(solution)/shard_map/all_to_all | solution.py:293
  53.1 1.6 %shard_map.129 = (bf16[128,512]{1,0:T(8,128)(2,1)}, bf16[128,512]{1,0:T(8,128)(2,1)}, bf16[128,512]{1,0:T(8,128)(2,1)}, bf16[128,512]{1,0:T(8,128)(2,1)}) custom-call(f32[320,128]{1,0:T(8,128)S(1)} %bitcast.15, f32[128,512]{1,0:T(8,128)S(1)} %get-tuple-element.26.fwd_ref, f32[128,512]{1,0:T(8,128)S(1)} %get-tuple-element.27.bwd_ref, ...), custom_call_target="tpu_custom_call" | custom-call | tf_op jit(solution)/shard_map/pallas_call | solution.py:281
  54.7 6.6 %all-to-all-done.2 = f32[8,1,128]{2,1,0:T(1,128)S(1)} async-done(((f32[8,1,128]{2,1,0:T(1,128)}), f32[8,1,128]{2,1,0:T(1,128)S(1)}, u32[]{:S(2)}, u32[]{:S(2)}) %all-to-all-start.2) | async-done | bytes 4128 | tf_op jit(solution)/shard_map/all_to_all | solution.py:293
  61.3 0.7 %shard_map.131 = (f32[16,512]{1,0:T(8,128)}, f32[16,512]{1,0:T(8,128)}, f32[1,512]{1,0:T(1,128)}) custom-call(f32[8,128]{1,0:T(8,128)S(1)} %bitcast.18, f32[16,512]{1,0:T(8,128)S(1)} %get-tuple-element.33.res_ref, f32[16,512]{1,0:T(8,128)S(1)} %get-tuple-element.34.log_ref, f32[1,512]{1,0:T(1,128)S(1)} %get-tuple-element.35.skip_ref), custom_call_target="tpu_custom_call" | custom-call | tf_op jit(solution)/shard_map/pallas_call | solution.py:281
Async XLA Ops:
  0.6 18.4 %copy-start.4 = (f32[16,512]{1,0:T(8,128)S(1)}, f32[16,512]{1,0:T(8,128)}, u32[]{:S(2)}) copy-start(f32[16,512]{1,0:T(8,128)} %rate_ref.3) | copy-start | bytes 98308
  0.6 18.5 %copy-start.5 = (f32[16,512]{1,0:T(8,128)S(1)}, f32[16,512]{1,0:T(8,128)}, u32[]{:S(2)}) copy-start(f32[16,512]{1,0:T(8,128)} %res_ref.3) | copy-start | bytes 98308
  0.7 18.6 %copy-start.6 = (f32[512]{0:T(512)S(1)}, f32[512]{0:T(512)}, u32[]{:S(2)}) copy-start(f32[512]{0:T(512)} %param.13) | copy-start | bytes 6148
  4.5 14.8 %copy-start.3 = (bf16[128,512]{1,0:T(8,128)(2,1)S(1)}, bf16[128,512]{1,0:T(8,128)(2,1)}, u32[]{:S(2)}) copy-start(bf16[128,512]{1,0:T(8,128)(2,1)} %grad_ref.3) | copy-start | bytes 393220
  4.5 14.8 %copy-start = (bf16[128,512]{1,0:T(8,128)(2,1)S(1)}, bf16[128,512]{1,0:T(8,128)(2,1)}, u32[]{:S(2)}) copy-start(bf16[128,512]{1,0:T(8,128)(2,1)} %key_ref.3) | copy-start | bytes 393220
  4.5 14.7 %copy-start.1 = (bf16[128,512]{1,0:T(8,128)(2,1)S(1)}, bf16[128,512]{1,0:T(8,128)(2,1)}, u32[]{:S(2)}) copy-start(bf16[128,512]{1,0:T(8,128)(2,1)} %value_ref.3) | copy-start | bytes 393220
  4.5 14.7 %copy-start.2 = (bf16[128,512]{1,0:T(8,128)(2,1)S(1)}, bf16[128,512]{1,0:T(8,128)(2,1)}, u32[]{:S(2)}) copy-start(bf16[128,512]{1,0:T(8,128)(2,1)} %gate_ref.3) | copy-start | bytes 393220
  4.5 25.8 %all-to-all-start = ((f32[448,1,128]{2,1,0:T(1,128)}), f32[448,1,128]{2,1,0:T(1,128)S(1)}, u32[]{:S(2)}, u32[]{:S(2)}) async-start(f32[448,1,128]{2,1,0:T(1,128)} %bitcast.1), calls=%async_computation | async-start | bytes 458752 | tf_op jit(solution)/shard_map/all_to_all | solution.py:293
  46.2 15.1 %all-to-all-start.2 = ((f32[8,1,128]{2,1,0:T(1,128)}), f32[8,1,128]{2,1,0:T(1,128)S(1)}, u32[]{:S(2)}, u32[]{:S(2)}) async-start(f32[8,1,128]{2,1,0:T(1,128)} %bitcast.8), calls=%async_computation.2 | async-start | bytes 8192 | tf_op jit(solution)/shard_map/all_to_all | solution.py:293

commit v3 on v2

--- a/solution.py
+++ b/solution.py
@@ -13,6 +13,9 @@
 ROWS_OUT = 7
 ROWS_BACK = 5
 Y_RUN = 4
+LEADS = (46, 46)
+ROOT_HIGH = 5
+GROUPS_AT_ONCE = 2
 VMEM = pl.BlockSpec(memory_space=pltpu.VMEM)
 PARAMS = pltpu.CompilerParams(vmem_limit_bytes=32 * 1024 * 1024)
 
@@ -46,49 +49,51 @@
     copies[4].wait()
     slope[...] = grad_ref[...].astype(jnp.float32) * gate_ref[...].astype(jnp.float32)
     zero = jnp.zeros((SUBLANES, LANES), jnp.float32)
-    keys = [(half, group) for half in range(halves) for group in range(groups)]
-
-    def advance(chunk, carry):
-        carry = list(carry)
-        x_tiles = [tile_of(mixed, chunk, group) for group in range(groups)]
-        z_tiles = [tile_of(slope, chunk, group) for group in range(groups)]
-        back_tiles = [tile_of(slope, block // SUBLANES - 1 - chunk, group) for group in range(groups)]
-        for inner in range(SUBLANES):
-            x_rows = [spread(tile, inner) for tile in x_tiles]
-            z_rows = [spread(tile, inner) for tile in z_tiles]
-            back_rows = [spread(tile, SUBLANES - 1 - inner) for tile in back_tiles]
-            for at, (half, group) in enumerate(keys):
-                state, timed, plain_sum, timed_sum, back, back_timed = carry[at]
-                step = steps[half, group]
-                moved = step * state
-                timed = step * timed + moved
-                state = moved + x_rows[group]
-                plain_sum = plain_sum + z_rows[group] * state
-                timed_sum = timed_sum + z_rows[group] * timed
-                back_moved = step * back
-                back_timed = step * back_timed + back_moved
-                back = back_moved + back_rows[group]
-                carry[at] = (state, timed, plain_sum, timed_sum, back, back_timed)
-        return tuple(carry)
-
-    done = lax.fori_loop(0, block // SUBLANES, advance, tuple((zero,) * 6 for _ in keys))
-    for at, (half, group) in enumerate(keys):
-        state, timed, plain_sum, timed_sum, back, back_timed = done[at]
-        step = steps[half, group]
-        base = (group * modes + half * SUBLANES) * ROWS_OUT
-        lanes = slice(group * LANES, (group + 1) * LANES)
-        skip_part = jnp.sum(mixed[:, lanes] * slope[:, lanes], axis=0, keepdims=True)
-        rows = (
-            step * state,
-            step * (timed + state),
-            back,
-            back_timed,
-            plain_sum,
-            timed_sum,
-            jnp.broadcast_to(skip_part, (SUBLANES, LANES)),
-        )
-        for row, value in enumerate(rows):
-            out_ref[pl.ds(base + row, SUBLANES, stride=ROWS_OUT), :] = value
+    for first in range(0, groups, GROUPS_AT_ONCE):
+        held = range(first, first + GROUPS_AT_ONCE)
+        keys = [(half, group) for half in range(halves) for group in held]
+
+        def advance(chunk, carry):
+            carry = list(carry)
+            x_tiles = {group: tile_of(mixed, chunk, group) for group in held}
+            z_tiles = {group: tile_of(slope, chunk, group) for group in held}
+            back_tiles = {group: tile_of(slope, block // SUBLANES - 1 - chunk, group) for group in held}
+            for inner in range(SUBLANES):
+                x_rows = {group: spread(x_tiles[group], inner) for group in held}
+                z_rows = {group: spread(z_tiles[group], inner) for group in held}
+                back_rows = {group: spread(back_tiles[group], SUBLANES - 1 - inner) for group in held}
+                for at, (half, group) in enumerate(keys):
+                    state, timed, plain_sum, timed_sum, back, back_timed = carry[at]
+                    step = steps[half, group]
+                    moved = step * state
+                    timed = step * timed + moved
+                    state = moved + x_rows[group]
+                    plain_sum = plain_sum + z_rows[group] * state
+                    timed_sum = timed_sum + z_rows[group] * timed
+                    back_moved = step * back
+                    back_timed = step * back_timed + back_moved
+                    back = back_moved + back_rows[group]
+                    carry[at] = (state, timed, plain_sum, timed_sum, back, back_timed)
+            return tuple(carry)
+
+        done = lax.fori_loop(0, block // SUBLANES, advance, tuple((zero,) * 6 for _ in keys))
+        for at, (half, group) in enumerate(keys):
+            state, timed, plain_sum, timed_sum, back, back_timed = done[at]
+            step = steps[half, group]
+            base = (group * modes + half * SUBLANES) * ROWS_OUT
+            lanes = slice(group * LANES, (group + 1) * LANES)
+            skip_part = jnp.sum(mixed[:, lanes] * slope[:, lanes], axis=0, keepdims=True)
+            rows = (
+                step * state,
+                step * (timed + state),
+                back,
+                back_timed,
+                plain_sum,
+                timed_sum,
+                jnp.broadcast_to(skip_part, (SUBLANES, LANES)),
+            )
+            for row, value in enumerate(rows):
+                out_ref[pl.ds(base + row, SUBLANES, stride=ROWS_OUT), :] = value
 
 
 def local_kernel(key_ref, value_ref, gate_ref, grad_ref, res_ref, rate_ref, skip_ref, fwd_ref, bwd_ref, before, after, taps):
@@ -151,8 +156,10 @@
     return jnp.where(keep, moved, 0.0)
 
 
-def scan_kernel(block, modes, in_ref, res_ref, rate_ref, out_ref):
+def scan_kernel(block, modes, lead, shift, in_ref, res_ref, rate_ref, out_ref):
     chunk = SUBLANES
+    turn, cut = divmod(-lead % (chunk * SUBLANES), chunk)
+    seam = lax.broadcasted_iota(jnp.int32, (SUBLANES, LANES), 0) == turn
     rate = jnp.broadcast_to(jnp.exp(rate_ref[...]), (SUBLANES, LANES))
     unit = jnp.sqrt(2.0 * rate / modes)
     amplitude = jnp.broadcast_to(res_ref[...], (SUBLANES, LANES)) * unit
@@ -166,6 +173,8 @@
     state, timed, back = zero, zero, zero
     states, timeds, backs = [], [], [None] * chunk
     for v in range(chunk):
+        if v == cut:
+            state, timed = jnp.where(seam, 0.0, state), jnp.where(seam, 0.0, timed)
         states.append(state)
         timeds.append(timed)
         moved = decay * state
@@ -174,6 +183,10 @@
     for v in reversed(range(chunk)):
         backs[v] = back
         back = decay * back + load(v, 2)
+        if v == cut:
+            back = jnp.where(seam, 0.0, back)
+    state, timed = (pltpu.roll(value, -turn % SUBLANES, 0) for value in (state, timed))
+    back = pltpu.roll(back, (SUBLANES - 1 - turn) % SUBLANES, 0)
     span = block * chunk
     distance = 1
     while distance < SUBLANES:
@@ -183,18 +196,24 @@
         state = state + older
         back = back + far * shifted(back, -distance)
         distance *= 2
-    state, timed, back = shifted(state, 1), shifted(timed, 1), shifted(back, -1)
+    state, timed = (pltpu.roll(value, (turn + 1) % SUBLANES, 0) for value in (state, timed))
+    back = pltpu.roll(back, turn, 0)
+    start_state, start_timed = jnp.where(seam, 0.0, state), jnp.where(seam, 0.0, timed)
+    end_back = jnp.where(seam, 0.0, back)
     plain, slow, skip = zero, zero, zero
     for v in range(chunk):
-        entering = states[v] + power[v] * state
-        entering_timed = timeds[v] + power[v] * (timed + float(block * v) * state)
-        leaving = backs[v] + power[chunk - 1 - v] * back
+        before, before_timed = (start_state, start_timed) if v >= cut else (state, timed)
+        entering = states[v] + power[v] * before
+        entering_timed = timeds[v] + power[v] * (before_timed + float(block * v) * before)
+        leaving = backs[v] + power[chunk - 1 - v] * (back if v >= cut else end_back)
         slope, slope_timed = load(v, 2), load(v, 3)
         plain = plain + load(v, 4) + slope * entering
         slow = slow + load(v, 5) + slope_timed * entering + slope * entering_timed
         skip = skip + load(v, 6)
-        out_ref[pl.ds(v * ROWS_BACK, SUBLANES, stride=chunk * ROWS_BACK), :] = entering
-        out_ref[pl.ds(v * ROWS_BACK + 1, SUBLANES, stride=chunk * ROWS_BACK), :] = leaving
+        rows, place = divmod(v + shift, chunk)
+        for row, value in ((0, entering), (1, leaving)):
+            value = pltpu.roll(value, rows % SUBLANES, 0) if rows % SUBLANES else value
+            out_ref[pl.ds(place * ROWS_BACK + row, SUBLANES, stride=chunk * ROWS_BACK), :] = value
 
     def total(value):
         return jnp.broadcast_to(jnp.sum(value, axis=0, keepdims=True), (SUBLANES, LANES))
@@ -207,22 +226,27 @@
             out_ref[pl.ds(v * ROWS_BACK + row, SUBLANES, stride=chunk * ROWS_BACK), :] = value
 
 
-def square_kernel(modes, in_ref, res_ref, log_ref, skip_ref, out_ref):
+def square_kernel(modes, shift, in_ref, res_ref, log_ref, skip_ref, out_ref):
     groups = res_ref.shape[1] // LANES
+    runs = groups * modes // SUBLANES
     total = jnp.zeros((SUBLANES, LANES), jnp.float32)
+    sublane = lax.broadcasted_iota(jnp.int32, (SUBLANES, LANES), 0)
+    skipped, turn = divmod(shift, SUBLANES)
+    for row, ref in ((2, res_ref), (3, log_ref)):
+        tiles = [in_ref[pl.ds(run * SUBLANES * ROWS_BACK + row, SUBLANES, stride=ROWS_BACK), :] for run in range(runs)]
+        if turn:
+            turned = [pltpu.roll(tile, SUBLANES - turn, 0) for tile in tiles]
+            tiles = [jnp.where(sublane < SUBLANES - turn, turned[run], turned[(run + 1) % runs]) for run in range(runs)]
+        for run in range(runs):
+            group, half = divmod(run, modes // SUBLANES)
+            value = tiles[(run + skipped) % runs]
+            ref[half * SUBLANES : (half + 1) * SUBLANES, group * LANES : (group + 1) * LANES] = value
+            total = total + value * value
     for group in range(groups):
-        lanes = slice(group * LANES, (group + 1) * LANES)
-        for half in range(modes // SUBLANES):
-            base = (group * modes + half * SUBLANES) * ROWS_BACK
-            rows = slice(half * SUBLANES, (half + 1) * SUBLANES)
-            for row, ref in ((2, res_ref), (3, log_ref)):
-                value = in_ref[pl.ds(base + row, SUBLANES, stride=ROWS_BACK), :]
-                ref[rows, lanes] = value
-                total = total + value * value
-        skip = in_ref[pl.ds(group * modes * ROWS_BACK + 4, 1), :]
-        skip_ref[:, lanes] = skip
-        first = lax.broadcasted_iota(jnp.int32, (SUBLANES, LANES), 0) == 0
-        total = total + jnp.where(first, skip * skip, 0.0)
+        at = (group * modes + shift) % (groups * modes)
+        skip = in_ref[pl.ds(at * ROWS_BACK + 4, 1), :]
+        skip_ref[:, group * LANES : (group + 1) * LANES] = skip
+        total = total + jnp.where(sublane == 0, skip * skip, 0.0)
     out_ref[...] = jnp.broadcast_to(jnp.sum(total, axis=0, keepdims=True), out_ref.shape)
 
 
@@ -234,7 +258,7 @@
     out_skip[...] = skip_ref[...] * factor
 
 
-def output_kernel(in_ref, fwd_ref, bwd_ref, key_ref, value_ref, gate_ref, grad_ref, res_ref, rate_ref, out_ref, gate_out, key_out, value_out):
+def output_kernel(shift, in_ref, fwd_ref, bwd_ref, key_ref, value_ref, gate_ref, grad_ref, res_ref, rate_ref, out_ref, gate_out, key_out, value_out):
     block, width = key_ref.shape
     modes = rate_ref.shape[0]
     groups = width // LANES
@@ -249,7 +273,7 @@
         back = [bwd_ref[c * SUBLANES : (c + 1) * SUBLANES, lanes] for c in range(chunks)]
         for mode in range(modes):
             one = slice(mode, mode + 1)
-            base = (group * modes + mode) * ROWS_BACK
+            base = (group * modes + mode + shift) % (groups * modes) * ROWS_BACK
             rate_row = jnp.broadcast_to(rate[one], (SUBLANES, LANES))
             jump = jnp.broadcast_to(stride[one], (SUBLANES, LANES))
             wave = jnp.broadcast_to(amplitude[one] * in_ref[pl.ds(base, 1), :], (SUBLANES, LANES)) * jnp.exp(-rate_row * within)
@@ -299,12 +323,28 @@
     groups = []
     for device in range(blocks):
         other = device ^ (2 * run)
-        groups.append([(other if shard % 2 else device) * shards + shard for shard in range(shards)])
+        members = [(other if shard % 2 else device) * shards + shard for shard in range(shards)]
+        groups.append(members[ROOT_HIGH:] + members[:ROOT_HIGH])
     return groups
 
 
 def floats(*shape):
     return jax.ShapeDtypeStruct(shape, jnp.float32)
+
+
+def summarize(key_in, value_in, gate_in, out_grad, log_rate):
+    block, width = key_in.shape
+    modes = log_rate.shape[0]
+    return call(
+        summary_kernel,
+        floats(modes * (width // LANES) * ROWS_OUT, LANES),
+        *in_hbm(key_in, value_in, gate_in, out_grad, log_rate),
+        scratch=[pltpu.VMEM((block, width), jnp.bfloat16)] * 4
+        + [pltpu.VMEM((modes, width), jnp.float32)]
+        + [pltpu.VMEM((block, width), jnp.float32)] * 2
+        + [pltpu.SemaphoreType.DMA((5,))],
+        space=pl.BlockSpec(memory_space=pltpu.HBM),
+    )
 
 
 def per_device(gate_in, key_in, value_in, out_grad, residue, log_rate, skip):
@@ -316,22 +356,18 @@
     owners = groups * modes
     assert owners == blocks
     device = lax.axis_index("seq")
-    own_mode, own_group = device % modes, device // modes
+    lead, reply_lead = LEADS
+    shift = (lead - reply_lead) % blocks
+    order = [(lead + at) % blocks for at in range(blocks)]
+    reply_order = [(reply_lead + at) % blocks for at in range(blocks)]
+    place = (device - lead) % blocks
+    own_mode, own_group = place % modes, place // modes
     own_rate = lax.dynamic_slice(log_rate, (own_mode, own_group * LANES), (1, LANES))
     own_res = lax.dynamic_slice(residue, (own_mode, own_group * LANES), (1, LANES))
     skip_row = skip.reshape(1, width)
 
-    sent = call(
-        summary_kernel,
-        floats(owners * ROWS_OUT, LANES),
-        *in_hbm(key_in, value_in, gate_in, out_grad, log_rate),
-        scratch=[pltpu.VMEM((block, width), jnp.bfloat16)] * 4
-        + [pltpu.VMEM((modes, width), jnp.float32)]
-        + [pltpu.VMEM((block, width), jnp.float32)] * 2
-        + [pltpu.SemaphoreType.DMA((5,))],
-        space=pl.BlockSpec(memory_space=pltpu.HBM),
-    )
-    arrived = exchange(sent, "seq")
+    sent = summarize(key_in, value_in, gate_in, out_grad, log_rate)
+    arrived = exchange(sent, "seq", [order])
     forward, backward = call(
         local_kernel,
         (floats(block, width), floats(block, width)),
@@ -344,19 +380,19 @@
     )
     arrived, forward, backward = lax.optimization_barrier((arrived, forward, backward))
     reply = call(
-        functools.partial(scan_kernel, block, modes),
+        functools.partial(scan_kernel, block, modes, lead, shift),
         floats(blocks * ROWS_BACK, LANES),
         arrived, own_res, own_rate,
     )
-    states = exchange(reply, "seq")
+    states = exchange(reply, "seq", [reply_order])
     raw_res, raw_log, raw_skip, squares = call(
-        functools.partial(square_kernel, modes),
+        functools.partial(square_kernel, modes, shift),
         (floats(modes, width), floats(modes, width), floats(1, width), floats(shards, LANES)),
         states,
     )
     squares = exchange(squares, ("seq", "chan"), near_groups(blocks, shards))
     gated_out, gate_grad, key_grad, value_grad = call(
-        output_kernel,
+        functools.partial(output_kernel, shift),
         (jax.ShapeDtypeStruct((block, width), jnp.bfloat16),) * 4,
         states, forward, backward, key_in, value_in, gate_in, out_grad, residue, log_rate,
     )

time: 62.3 us -> 56 us (0.90)
  the two profiles are of different devices: /device:TPU:8 before, /device:TPU:56 now
where the time goes in v3:
time: 56 us; the launch traced here: 55.7 us
  starting transfers between devices  20.3 us (36%)
  blocking collectives  15 us (27%)
  waiting for transfers between devices  9.46 us (17%)
  Pallas kernels  9.43 us (17%)
  local copies, waits for them, and re-layouts  0.78 us (1%)
  between operations  0.78 us (1%)
    all_to_all x2, starting transfers between devices, exchange(): lax.all_to_all(rows.reshape(count, 1, lanes), axis, 0, 0, axis_index_grou...  20.3 us
    all_to_all x1, blocking collectives, exchange(): lax.all_to_all(rows.reshape(count, 1, lanes), axis, 0, 0, axis_index_grou...  15 us
    all_to_all x2, waiting for transfers between devices, exchange(): lax.all_to_all(rows.reshape(count, 1, lanes), axis, 0, 0, axis_index_grou...  9.46 us
    pallas_call x6, Pallas kernels, call(): pl.pallas_call(kernel, out_shape=out_shape, in_specs=[space] * len(args),...  9.43 us
  transfers between devices with their start and end apart: 2, of which 2 were waited for; matrix products, arithmetic and copies ran while one was open for 0% of the time, Pallas kernels for 8%

profile of v3, /device:TPU:56, one launch (start us, length us, event | category | flops | bytes accessed | tf_op | source)
XLA Modules:
  0.0 55.7 jit_solution(438745489603662152)
XLA Ops:
  0.6 0.0 copy-start.4
  0.6 0.0 copy-start.5
  0.7 3.7 %shard_map.126 = f32[448,128]{1,0:T(8,128)} custom-call(bf16[128,512]{1,0:T(8,128)(2,1)} %key_ref.3, bf16[128,512]{1,0:T(8,128)(2,1)} %value_ref.3, bf16[128,512]{1,0:T(8,128)(2,1)} %gate_ref.3, bf16[128,512]{1,0:T(8,128)(2,1)} %grad_ref.3, f32[16,512]{1,0:T(8,128)} %rate_ref.3), custom_call_target="tpu_custom_call" | custom-call | tf_op jit(solution)/shard_map/pallas_call | solution.py:305
  4.4 0.0 copy-start
  4.4 0.0 copy-start.1
  4.4 0.0 copy-start.2
  4.4 0.0 copy-start.3
  4.4 14.0 %all-to-all-start = ((f32[448,1,128]{2,1,0:T(1,128)}), f32[448,1,128]{2,1,0:T(1,128)S(1)}, u32[]{:S(2)}, u32[]{:S(2)}) async-start(f32[448,1,128]{2,1,0:T(1,128)} %bitcast.1), calls=%async_computation | async-start | bytes 458752 | tf_op jit(solution)/shard_map/all_to_all | solution.py:317
  18.5 0.0 copy-done.4
  18.5 0.1 dynamic_slice.7.rate_ref
  18.6 0.0 copy-done.5
  18.6 0.0 copy-start.6
  18.6 0.1 dynamic_slice.6.res_ref
  18.7 0.0 copy-done
  18.7 0.0 copy-done.1
  18.7 0.0 copy-done.2
  18.7 0.0 copy-done.3
  18.7 0.6 %copy-done.6 = f32[512]{0:T(512)S(1)} copy-done((f32[512]{0:T(512)S(1)}, f32[512]{0:T(512)}, u32[]{:S(2)}) %copy-start.6) | copy-done | bytes 2072
  19.3 2.7 %shard_map.127 = (f32[128,512]{1,0:T(8,128)S(1)}, f32[128,512]{1,0:T(8,128)S(1)}) custom-call(bf16[128,512]{1,0:T(8,128)(2,1)S(1)} %copy-done, bf16[128,512]{1,0:T(8,128)(2,1)S(1)} %copy-done.1, bf16[128,512]{1,0:T(8,128)(2,1)S(1)} %copy-done.2, bf16[128,512]{1,0:T(8,128)(2,1)S(1)} %copy-done.3, f32[16,512]{1,0:T(8,128)S(1)} %copy-done.5, ...), custom_call_target="tpu_custom_call" | custom-call | tf_op jit(solution)/shard_map/pallas_call | solution.py:305
  22.0 5.8 %all-to-all-done = f32[448,1,128]{2,1,0:T(1,128)S(1)} async-done(((f32[448,1,128]{2,1,0:T(1,128)}), f32[448,1,128]{2,1,0:T(1,128)S(1)}, u32[]{:S(2)}, u32[]{:S(2)}) %all-to-all-start) | async-done | bytes 229408 | tf_op jit(solution)/shard_map/all_to_all | solution.py:317
  27.8 0.1 shard_map.128
  27.9 15.0 %all_to_all.15 = f32[320,1,128]{2,1,0:T(1,128)S(1)} all-to-all(f32[320,1,128]{2,1,0:T(1,128)S(1)} %bitcast.17), channel_id=1, replica_groups={{368,376,384,392,400,408,416,424,432,440,448,456,464,472,480,488,496,50..., dimensions={0} | all-to-all | bytes 327680 | tf_op jit(solution)/shard_map/all_to_all | solution.py:317
  42.9 0.6 %shard_map.130 = (f32[16,512]{1,0:T(8,128)S(1)}, f32[16,512]{1,0:T(8,128)S(1)}, f32[1,512]{1,0:T(1,128)S(1)}, f32[8,128]{1,0:T(8,128)}) custom-call(f32[320,128]{1,0:T(8,128)S(1)} %bitcast.14), custom_call_target="tpu_custom_call" | custom-call | tf_op jit(solution)/shard_map/pallas_call | solution.py:305
  43.5 6.3 %all-to-all-start.2 = ((f32[8,1,128]{2,1,0:T(1,128)}), f32[8,1,128]{2,1,0:T(1,128)S(1)}, u32[]{:S(2)}, u32[]{:S(2)}) async-start(f32[8,1,128]{2,1,0:T(1,128)} %bitcast.8), calls=%async_computation.2 | async-start | bytes 8192 | tf_op jit(solution)/shard_map/all_to_all | solution.py:317
  49.8 1.6 %shard_map.129 = (bf16[128,512]{1,0:T(8,128)(2,1)}, bf16[128,512]{1,0:T(8,128)(2,1)}, bf16[128,512]{1,0:T(8,128)(2,1)}, bf16[128,512]{1,0:T(8,128)(2,1)}) custom-call(f32[320,128]{1,0:T(8,128)S(1)} %bitcast.15, f32[128,512]{1,0:T(8,128)S(1)} %get-tuple-element.26.fwd_ref, f32[128,512]{1,0:T(8,128)S(1)} %get-tuple-element.27.bwd_ref, ...), custom_call_target="tpu_custom_call" | custom-call | tf_op jit(solution)/shard_map/pallas_call | solution.py:305
  51.3 3.7 %all-to-all-done.2 = f32[8,1,128]{2,1,0:T(1,128)S(1)} async-done(((f32[8,1,128]{2,1,0:T(1,128)}), f32[8,1,128]{2,1,0:T(1,128)S(1)}, u32[]{:S(2)}, u32[]{:S(2)}) %all-to-all-start.2) | async-done | bytes 4128 | tf_op jit(solution)/shard_map/all_to_all | solution.py:317
  55.0 0.7 %shard_map.131 = (f32[16,512]{1,0:T(8,128)}, f32[16,512]{1,0:T(8,128)}, f32[1,512]{1,0:T(1,128)}) custom-call(f32[8,128]{1,0:T(8,128)S(1)} %bitcast.18, f32[16,512]{1,0:T(8,128)S(1)} %get-tuple-element.33.res_ref, f32[16,512]{1,0:T(8,128)S(1)} %get-tuple-element.34.log_ref, f32[1,512]{1,0:T(1,128)S(1)} %get-tuple-element.35.skip_ref), custom_call_target="tpu_custom_call" | custom-call | tf_op jit(solution)/shard_map/pallas_call | solution.py:305
Async XLA Ops:
  0.6 17.9 %copy-start.4 = (f32[16,512]{1,0:T(8,128)S(1)}, f32[16,512]{1,0:T(8,128)}, u32[]{:S(2)}) copy-start(f32[16,512]{1,0:T(8,128)} %rate_ref.3) | copy-start | bytes 98308
  0.6 17.9 %copy-start.5 = (f32[16,512]{1,0:T(8,128)S(1)}, f32[16,512]{1,0:T(8,128)}, u32[]{:S(2)}) copy-start(f32[16,512]{1,0:T(8,128)} %res_ref.3) | copy-start | bytes 98308
  4.4 14.3 %copy-start = (bf16[128,512]{1,0:T(8,128)(2,1)S(1)}, bf16[128,512]{1,0:T(8,128)(2,1)}, u32[]{:S(2)}) copy-start(bf16[128,512]{1,0:T(8,128)(2,1)} %key_ref.3) | copy-start | bytes 393220
  4.4 14.3 %copy-start.1 = (bf16[128,512]{1,0:T(8,128)(2,1)S(1)}, bf16[128,512]{1,0:T(8,128)(2,1)}, u32[]{:S(2)}) copy-start(bf16[128,512]{1,0:T(8,128)(2,1)} %value_ref.3) | copy-start | bytes 393220
  4.4 14.3 %copy-start.2 = (bf16[128,512]{1,0:T(8,128)(2,1)S(1)}, bf16[128,512]{1,0:T(8,128)(2,1)}, u32[]{:S(2)}) copy-start(bf16[128,512]{1,0:T(8,128)(2,1)} %gate_ref.3) | copy-start | bytes 393220
  4.4 14.3 %copy-start.3 = (bf16[128,512]{1,0:T(8,128)(2,1)S(1)}, bf16[128,512]{1,0:T(8,128)(2,1)}, u32[]{:S(2)}) copy-start(bf16[128,512]{1,0:T(8,128)(2,1)} %grad_ref.3) | copy-start | bytes 393220
  4.4 23.4 %all-to-all-start = ((f32[448,1,128]{2,1,0:T(1,128)}), f32[448,1,128]{2,1,0:T(1,128)S(1)}, u32[]{:S(2)}, u32[]{:S(2)}) async-start(f32[448,1,128]{2,1,0:T(1,128)} %bitcast.1), calls=%async_computation | async-start | bytes 458752 | tf_op jit(solution)/shard_map/all_to_all | solution.py:317
  18.6 0.7 %copy-start.6 = (f32[512]{0:T(512)S(1)}, f32[512]{0:T(512)}, u32[]{:S(2)}) copy-start(f32[512]{0:T(512)} %param.13) | copy-start | bytes 6148
  43.5 11.5 %all-to-all-start.2 = ((f32[8,1,128]{2,1,0:T(1,128)}), f32[8,1,128]{2,1,0:T(1,128)S(1)}, u32[]{:S(2)}, u32[]{:S(2)}) async-start(f32[8,1,128]{2,1,0:T(1,128)} %bitcast.8), calls=%async_computation.2 | async-start | bytes 8192 | tf_op jit(solution)/shard_map/all_to_all | solution.py:317

commit v4 on v3

v4 whole, which is shorter than its diff:
```python
import functools

import jax
import jax.numpy as jnp
from jax import lax
from jax.experimental import pallas as pl
from jax.experimental.pallas import tpu as pltpu
from jax.sharding import PartitionSpec as P

CLIP_RMS = 1.0
LANES = 128
SUBLANES = 8
ROWS_OUT = 7
ROWS_BACK = 5
Y_RUN = 4
LEAD = 46
ROOT_HIGH = 5
PART = 16
GROUPS_AT_ONCE = 2
VMEM = pl.BlockSpec(memory_space=pltpu.VMEM)
PARAMS = pltpu.CompilerParams(vmem_limit_bytes=32 * 1024 * 1024)


def tile_of(ref, chunk, group):
    return ref[pl.ds(pl.multiple_of(chunk * SUBLANES, SUBLANES), SUBLANES), group * LANES : (group + 1) * LANES]


def spread(tile, row):
    return jnp.broadcast_to(tile[row : row + 1], (SUBLANES, LANES))


def summary_kernel(key_hbm, value_hbm, gate_hbm, grad_hbm, rate_hbm, skip_hbm, out_ref, ahead_ref, behind_ref, skip_ref, key_ref, value_ref, gate_ref, grad_ref, rate_ref, mixed, slope, sems):
    block, width = key_ref.shape
    modes = rate_ref.shape[0]
    halves, groups = modes // SUBLANES, width // LANES
    pairs = ((rate_hbm, rate_ref), (key_hbm, key_ref), (value_hbm, value_ref), (grad_hbm, grad_ref), (gate_hbm, gate_ref), (skip_hbm, skip_ref))
    copies = [pltpu.make_async_copy(source, target, sems.at[at]) for at, (source, target) in enumerate(pairs)]
    for copy in copies:
        copy.start()
    copies[0].wait()
    steps = {}
    for half in range(halves):
        for group in range(groups):
            rate = jnp.exp(rate_ref[half * SUBLANES : (half + 1) * SUBLANES, group * LANES : (group + 1) * LANES])
            steps[half, group] = jnp.exp(-rate)
    copies[1].wait()
    copies[2].wait()
    mixed[...] = key_ref[...].astype(jnp.float32) * value_ref[...].astype(jnp.float32)
    copies[3].wait()
    copies[4].wait()
    slope[...] = grad_ref[...].astype(jnp.float32) * gate_ref[...].astype(jnp.float32)
    copies[5].wait()
    zero = jnp.zeros((SUBLANES, LANES), jnp.float32)
    for first in range(0, groups, GROUPS_AT_ONCE):
        held = range(first, first + GROUPS_AT_ONCE)
        keys = [(half, group) for half in range(halves) for group in held]

        def advance(part, carry):
            carry = list(carry)
            for at, (half, group) in enumerate(keys):
                rows = slice(half * SUBLANES, (half + 1) * SUBLANES)
                lanes = slice(group * LANES, (group + 1) * LANES)
                ahead_ref[part, rows, lanes] = carry[at][0]
                behind_ref[block // PART - 1 - part, rows, lanes] = carry[at][4]
            for piece in range(PART // SUBLANES):
                chunk = part * (PART // SUBLANES) + piece
                x_tiles = {group: tile_of(mixed, chunk, group) for group in held}
                z_tiles = {group: tile_of(slope, chunk, group) for group in held}
                back_tiles = {group: tile_of(slope, block // SUBLANES - 1 - chunk, group) for group in held}
                for inner in range(SUBLANES):
                    x_rows = {group: spread(x_tiles[group], inner) for group in held}
                    z_rows = {group: spread(z_tiles[group], inner) for group in held}
                    back_rows = {group: spread(back_tiles[group], SUBLANES - 1 - inner) for group in held}
                    for at, (half, group) in enumerate(keys):
                        state, timed, plain_sum, timed_sum, back, back_timed = carry[at]
                        step = steps[half, group]
                        moved = step * state
                        timed = step * timed + moved
                        state = moved + x_rows[group]
                        plain_sum = plain_sum + z_rows[group] * state
                        timed_sum = timed_sum + z_rows[group] * timed
                        back_moved = step * back
                        back_timed = step * back_timed + back_moved
                        back = back_moved + back_rows[group]
                        carry[at] = (state, timed, plain_sum, timed_sum, back, back_timed)
            return tuple(carry)

        done = lax.fori_loop(0, block // PART, advance, tuple((zero,) * 6 for _ in keys))
        for at, (half, group) in enumerate(keys):
            state, timed, plain_sum, timed_sum, back, back_timed = done[at]
            step = steps[half, group]
            base = (group * modes + half * SUBLANES) * ROWS_OUT
            lanes = slice(group * LANES, (group + 1) * LANES)
            skip_part = jnp.sum(mixed[:, lanes] * slope[:, lanes], axis=0, keepdims=True)
            rows = (
                step * state,
                step * (timed + state),
                back,
                back_timed,
                plain_sum,
                timed_sum,
                jnp.broadcast_to(skip_part, (SUBLANES, LANES)),
            )
            for row, value in enumerate(rows):
                out_ref[pl.ds(base + row, SUBLANES, stride=ROWS_OUT), :] = value


def shifted(value, amount):
    rows = lax.broadcasted_iota(jnp.int32, value.shape, 0)
    moved = pltpu.roll(value, amount % value.shape[0], 0)
    keep = rows >= amount if amount > 0 else rows < value.shape[0] + amount
    return jnp.where(keep, moved, 0.0)


def scan_kernel(block, modes, lead, in_ref, res_ref, rate_ref, out_ref):
    chunk = SUBLANES
    turn, cut = divmod(-lead % (chunk * SUBLANES), chunk)
    seam = lax.broadcasted_iota(jnp.int32, (SUBLANES, LANES), 0) == turn
    blocks = chunk * SUBLANES
    place = lax.rem(lax.axis_index("seq") + (blocks - lead), blocks)
    own_mode, own_group = lax.rem(place, modes), lax.div(place, modes)
    rows = lax.broadcasted_iota(jnp.int32, (modes, LANES), 0)

    def own(ref):
        picked = jnp.zeros((modes, LANES), jnp.float32)
        for group in range(ref.shape[1] // LANES):
            mine = rows == jnp.where(own_group == group, own_mode, -1)
            picked = jnp.where(mine, ref[:, group * LANES : (group + 1) * LANES], picked)
        return jnp.broadcast_to(jnp.sum(picked, axis=0, keepdims=True), (SUBLANES, LANES))

    rate = jnp.exp(own(rate_ref))
    unit = jnp.sqrt(2.0 * rate / modes)
    amplitude = own(res_ref) * unit
    power = [jnp.exp(-float(block * v) * rate) for v in range(chunk)]
    decay = power[1]

    def load(v, row):
        return in_ref[pl.ds(v * ROWS_OUT + row, SUBLANES, stride=chunk * ROWS_OUT), :]

    zero = jnp.zeros((SUBLANES, LANES), jnp.float32)
    state, timed, back = zero, zero, zero
    states, timeds, backs = [], [], [None] * chunk
    for v in range(chunk):
        if v == cut:
            state, timed = jnp.where(seam, 0.0, state), jnp.where(seam, 0.0, timed)
        states.append(state)
        timeds.append(timed)
        moved = decay * state
        timed = decay * timed + float(block) * moved + load(v, 1)
        state = moved + load(v, 0)
    for v in reversed(range(chunk)):
        backs[v] = back
        back = decay * back + load(v, 2)
        if v == cut:
            back = jnp.where(seam, 0.0, back)
    state, timed = (pltpu.roll(value, -turn % SUBLANES, 0) for value in (state, timed))
    back = pltpu.roll(back, (SUBLANES - 1 - turn) % SUBLANES, 0)
    span = block * chunk
    distance = 1
    while distance < SUBLANES:
        far = jnp.exp(-float(span * distance) * rate)
        older = far * shifted(state, distance)
        timed = timed + far * shifted(timed, distance) + float(span * distance) * older
        state = state + older
        back = back + far * shifted(back, -distance)
        distance *= 2
    state, timed = (pltpu.roll(value, (turn + 1) % SUBLANES, 0) for value in (state, timed))
    back = pltpu.roll(back, turn, 0)
    start_state, start_timed = jnp.where(seam, 0.0, state), jnp.where(seam, 0.0, timed)
    end_back = jnp.where(seam, 0.0, back)
    plain, slow, skip = zero, zero, zero
    for v in range(chunk):
        before, before_timed = (start_state, start_timed) if v >= cut else (state, timed)
        entering = states[v] + power[v] * before
        entering_timed = timeds[v] + power[v] * (before_timed + float(block * v) * before)
        leaving = backs[v] + power[chunk - 1 - v] * (back if v >= cut else end_back)
        slope, slope_timed = load(v, 2), load(v, 3)
        plain = plain + load(v, 4) + slope * entering
        slow = slow + load(v, 5) + slope_timed * entering + slope * entering_timed
        skip = skip + load(v, 6)
        for row, value in ((0, entering), (1, leaving)):
            out_ref[pl.ds(v * ROWS_BACK + row, SUBLANES, stride=chunk * ROWS_BACK), :] = value

    def total(value):
        return jnp.broadcast_to(jnp.sum(value, axis=0, keepdims=True), (SUBLANES, LANES))

    plain, slow, skip = total(plain), total(slow), total(skip)
    raw_res = plain * unit
    raw_log = (0.5 * plain - rate * slow) * amplitude
    for v in range(chunk):
        for row, value in ((2, raw_res), (3, raw_log), (4, skip)):
            out_ref[pl.ds(v * ROWS_BACK + row, SUBLANES, stride=chunk * ROWS_BACK), :] = value


def square_kernel(modes, in_ref, res_ref, log_ref, skip_ref, out_ref):
    groups = res_ref.shape[1] // LANES
    first = lax.broadcasted_iota(jnp.int32, (SUBLANES, LANES), 0) == 0
    total = jnp.zeros((SUBLANES, LANES), jnp.float32)
    for group in range(groups):
        lanes = slice(group * LANES, (group + 1) * LANES)
        for half in range(modes // SUBLANES):
            base = (group * modes + half * SUBLANES) * ROWS_BACK
            for row, ref in ((2, res_ref), (3, log_ref)):
                value = in_ref[pl.ds(base + row, SUBLANES, stride=ROWS_BACK), :]
                ref[half * SUBLANES : (half + 1) * SUBLANES, lanes] = value
                total = total + value * value
        skip = in_ref[pl.ds(group * modes * ROWS_BACK + 4, 1), :]
        skip_ref[:, lanes] = skip
        total = total + jnp.where(first, skip * skip, 0.0)
    out_ref[...] = jnp.broadcast_to(jnp.sum(total, axis=0, keepdims=True), out_ref.shape)


def output_kernel(count, in_ref, squares_ref, raw_res_ref, raw_log_ref, raw_skip_ref, ahead_ref, behind_ref, key_ref, value_ref, gate_ref, grad_ref, res_ref, rate_ref, skip_ref, out_hbm, gate_hbm, key_hbm, value_hbm, res_hbm, log_hbm, gain_hbm, out_ref, gate_out, key_out, value_out, mixed, slope, entering, leaving, taps, res_out, log_out, gain_out, sems, clip_sems):
    block, width = key_ref.shape
    modes = rate_ref.shape[0]
    groups = width // LANES
    parts, halves = block // PART, modes // SUBLANES
    tile = (SUBLANES, LANES)
    zero = jnp.zeros(tile, jnp.float32)
    place = lax.broadcasted_iota(jnp.int32, tile, 0)
    odd, second, fourth = ((place & bit) != 0 for bit in (1, 2, 4))

    def row(ref, at):
        return jnp.broadcast_to(ref[at : at + 1, :], tile)

    squares = jnp.sum(jnp.sum(squares_ref[...], axis=0, keepdims=True), axis=1, keepdims=True)
    factor = CLIP_RMS / jnp.maximum(jnp.sqrt(squares / count), CLIP_RMS)
    copies = []
    for at, (raw, held, target) in enumerate(
        ((raw_res_ref, res_out, res_hbm), (raw_log_ref, log_out, log_hbm), (raw_skip_ref, gain_out, gain_hbm))
    ):
        held[...] = raw[...] * factor
        copies.append(pltpu.make_async_copy(held, target, clip_sems.at[at]))
        copies[-1].start()

    def leave(group, first, *pairs):
        lanes = slice(group * LANES, (group + 1) * LANES)
        for at, (source, target) in enumerate(pairs):
            copies.append(pltpu.make_async_copy(source.at[:, lanes], target.at[:, lanes], sems.at[group, first + at]))
            copies[-1].start()

    for group in range(groups):
        lanes = slice(group * LANES, (group + 1) * LANES)
        for part in range(parts):
            at, rows = part * (PART + SUBLANES), slice(part * PART, (part + 1) * PART)
            for ref in (mixed, slope):
                ref[at : at + SUBLANES, :] = zero
            start = at + SUBLANES
            mixed[start : start + PART, :] = key_ref[rows, lanes].astype(jnp.float32) * value_ref[rows, lanes].astype(jnp.float32)
            slope[start : start + PART, :] = grad_ref[rows, lanes].astype(jnp.float32) * gate_ref[rows, lanes].astype(jnp.float32)
        for ref in (mixed, slope):
            ref[parts * (PART + SUBLANES) :, :] = zero
        powers = []
        for half in range(halves):
            rows = slice(half * SUBLANES, (half + 1) * SUBLANES)
            rate = jnp.exp(rate_ref[rows, lanes])
            amplitude = res_ref[rows, lanes] * jnp.sqrt(2.0 * rate / modes)
            step, leap = jnp.exp(-rate), jnp.exp(-float(PART) * rate)
            square = step * step
            powers.append((amplitude, step, square, square * square, jnp.exp(-float(SUBLANES) * rate)))
            base = (group * modes + half * SUBLANES) * ROWS_BACK
            wave = in_ref[pl.ds(base, SUBLANES, stride=ROWS_BACK), :]
            echo = in_ref[pl.ds(base + 1, SUBLANES, stride=ROWS_BACK), :]
            for part in range(parts):
                mirror = parts - 1 - part
                at, mirrored = part * modes + half * SUBLANES, mirror * modes + half * SUBLANES
                entering[at : at + SUBLANES, :] = amplitude * (step * ahead_ref[part, rows, lanes] + wave)
                leaving[mirrored : mirrored + SUBLANES, :] = amplitude * (behind_ref[mirror, rows, lanes] + echo)
                if part + 1 < parts:
                    wave, echo = wave * leap, echo * leap
        ahead, back = [zero] * (2 * parts), [zero] * (2 * parts)
        near, far = zero, zero
        for mode in range(modes):
            half, inner = divmod(mode, SUBLANES)
            amplitude, step, square, fourth_power, jump = (spread(power, inner) for power in powers[half])
            up = jnp.where(odd, step, 1.0) * jnp.where(second, square, 1.0) * jnp.where(fourth, fourth_power, 1.0)
            down = step * jnp.where(odd, 1.0, step) * jnp.where(second, 1.0, square) * jnp.where(fourth, 1.0, fourth_power)
            tap = amplitude * up
            near, far = near + tap, far + tap * jump
            for part in range(parts):
                wave = row(entering, part * modes + mode) * up
                echo = row(leaving, part * modes + mode) * down
                ahead[2 * part] = ahead[2 * part] + wave
                ahead[2 * part + 1] = ahead[2 * part + 1] + wave * jump
                back[2 * part + 1] = back[2 * part + 1] + echo
                back[2 * part] = back[2 * part] + echo * jump
        taps[0:SUBLANES, :] = near
        taps[SUBLANES:, :] = far
        skip_row = jnp.broadcast_to(skip_ref[:, lanes], tile)
        for shift in range(SUBLANES):
            close, apart = row(taps, shift), row(taps, SUBLANES + shift)
            if shift == 0:
                close = close + skip_row
            for part in range(parts):
                start = part * (PART + SUBLANES) + SUBLANES
                low = mixed[pl.ds(start - shift, SUBLANES), :]
                high = mixed[pl.ds(start + SUBLANES - shift, SUBLANES), :]
                ahead[2 * part] = ahead[2 * part] + close * low
                ahead[2 * part + 1] = ahead[2 * part + 1] + (close * high + apart * low)
        for pair in range(parts):
            rows = slice(pair * PART, (pair + 1) * PART)
            filtered = jnp.concatenate([ahead[2 * pair], ahead[2 * pair + 1]], axis=0)
            out_ref[rows, lanes] = (gate_ref[rows, lanes].astype(jnp.float32) * filtered).astype(jnp.bfloat16)
            gate_out[rows, lanes] = (grad_ref[rows, lanes].astype(jnp.float32) * filtered).astype(jnp.bfloat16)
        leave(group, 0, (out_ref, out_hbm), (gate_out, gate_hbm))
        for shift in range(SUBLANES):
            close, apart = row(taps, shift), row(taps, SUBLANES + shift)
            if shift == 0:
                close = close + skip_row
            for part in range(parts):
                start = part * (PART + SUBLANES) + SUBLANES
                low = slope[pl.ds(start + shift, SUBLANES), :]
                high = slope[pl.ds(start + SUBLANES + shift, SUBLANES), :]
                back[2 * part] = back[2 * part] + (close * low + apart * high)
                back[2 * part + 1] = back[2 * part + 1] + close * high
        for pair in range(parts):
            rows = slice(pair * PART, (pair + 1) * PART)
            mixed_grad = jnp.concatenate([back[2 * pair], back[2 * pair + 1]], axis=0)
            key_out[rows, lanes] = (value_ref[rows, lanes].astype(jnp.float32) * mixed_grad).astype(jnp.bfloat16)
            value_out[rows, lanes] = (key_ref[rows, lanes].astype(jnp.float32) * mixed_grad).astype(jnp.bfloat16)
        leave(group, 2, (key_out, key_hbm), (value_out, value_hbm))
    for copy in copies:
        copy.wait()


def in_hbm(*arrays):
    return tuple(pltpu.with_memory_space_constraint(array, pltpu.HBM) for array in arrays)


def call(kernel, out_shape, *args, scratch=(), space=VMEM, out_space=VMEM):
    multiple = isinstance(out_shape, (tuple, list))
    return pl.pallas_call(
        kernel,
        out_shape=out_shape,
        in_specs=[space] * len(args),
        out_specs=[out_space] * len(out_shape) if multiple else out_space,
        scratch_shapes=list(scratch),
        compiler_params=PARAMS,
    )(*args)


def exchange(rows, axis, groups=None):
    count, lanes = rows.shape
    moved = lax.all_to_all(rows.reshape(count, 1, lanes), axis, 0, 0, axis_index_groups=groups, tiled=True)
    return moved.reshape(count, lanes)


def near_groups(blocks, shards):
    run = blocks // Y_RUN
    groups = []
    for device in range(blocks):
        other = device ^ (2 * run)
        members = [(other if shard % 2 else device) * shards + shard for shard in range(shards)]
        groups.append(members[ROOT_HIGH:] + members[:ROOT_HIGH])
    return groups


def floats(*shape):
    return jax.ShapeDtypeStruct(shape, jnp.float32)


def summarize(key_in, value_in, gate_in, out_grad, log_rate, skip):
    block, width = key_in.shape
    modes = log_rate.shape[0]
    return call(
        summary_kernel,
        (
            floats(modes * (width // LANES) * ROWS_OUT, LANES),
            floats(block // PART, modes, width),
            floats(block // PART, modes, width),
            floats(1, width),
        ),
        *in_hbm(key_in, value_in, gate_in, out_grad, log_rate, skip),
        scratch=[pltpu.VMEM((block, width), jnp.bfloat16)] * 4
        + [pltpu.VMEM((modes, width), jnp.float32)]
        + [pltpu.VMEM((block, width), jnp.float32)] * 2
        + [pltpu.SemaphoreType.DMA((6,))],
        space=pl.BlockSpec(memory_space=pltpu.HBM),
    )


def finish(states, squares, raw_res, raw_log, raw_skip, ahead, behind, key_in, value_in, gate_in, out_grad, residue, log_rate, skip_row):
    block, width = key_in.shape
    modes, groups, shards = residue.shape[0], width // LANES, squares.shape[0]
    return call(
        functools.partial(output_kernel, float((2 * modes + 1) * width * shards)),
        (jax.ShapeDtypeStruct((block, width), jnp.bfloat16),) * 4 + (floats(modes, width), floats(modes, width), floats(1, width)),
        states, squares, raw_res, raw_log, raw_skip, ahead, behind, key_in, value_in, gate_in, out_grad, residue, log_rate, skip_row,
        out_space=pl.BlockSpec(memory_space=pl.ANY),
        scratch=[pltpu.VMEM((block, width), jnp.bfloat16)] * 4
        + [pltpu.VMEM((block // PART * (PART + SUBLANES) + SUBLANES, LANES), jnp.float32)] * 2
        + [pltpu.VMEM((block // PART * modes, LANES), jnp.float32)] * 2
        + [pltpu.VMEM((PART, LANES), jnp.float32)]
        + [pltpu.VMEM((modes, width), jnp.float32)] * 2
        + [pltpu.VMEM((1, width), jnp.float32), pltpu.SemaphoreType.DMA((groups, 4)), pltpu.SemaphoreType.DMA((3,))],
    )


def per_device(gate_in, key_in, value_in, out_grad, residue, log_rate, skip):
    block, width = gate_in.shape
    modes = residue.shape[0]
    blocks = lax.axis_size("seq")
    shards = lax.axis_size("chan")
    groups = width // LANES
    owners = groups * modes
    assert owners == blocks
    order = [(LEAD + at) % blocks for at in range(blocks)]

    sent, ahead, behind, skip_row = summarize(key_in, value_in, gate_in, out_grad, log_rate, skip.reshape(1, width))
    arrived = exchange(sent, "seq", [order])
    reply = call(
        functools.partial(scan_kernel, block, modes, LEAD),
        floats(blocks * ROWS_BACK, LANES),
        arrived, residue, log_rate,
    )
    states = exchange(reply, "seq", [order])
    raw_res, raw_log, raw_skip, squares = call(
        functools.partial(square_kernel, modes),
        (floats(modes, width), floats(modes, width), floats(1, width), floats(shards, LANES)),
        states,
    )
    squares = exchange(squares, ("seq", "chan"), near_groups(blocks, shards))
    gated_out, gate_grad, key_grad, value_grad, residue_grad, log_rate_grad, skip_grad = finish(
        states, squares, raw_res, raw_log, raw_skip, ahead, behind, key_in, value_in, gate_in, out_grad, residue, log_rate, skip_row
    )
    return gated_out, gate_grad, key_grad, value_grad, residue_grad, log_rate_grad, skip_grad.reshape(width)


def solution(mesh):
    field, parameter, gain = P("seq", "chan"), P(None, "chan"), P("chan")
    return jax.shard_map(
        per_device,
        mesh=mesh,
        in_specs=(field, field, field, field, parameter, parameter, gain),
        out_specs=(field, field, field, field, parameter, parameter, gain),
        check_vma=False,
    )
```

time: 56 us -> 55.4 us (0.989)
  blocking collectives: 15 us -> 48.8 us
  starting transfers between devices: 20.3 us -> 0 us
  waiting for transfers between devices: 9.46 us -> 0 us
  Pallas kernels: 9.43 us -> 5.56 us
  local copies, waits for them, and re-layouts: 0.78 us -> 0.03 us
    all_to_all x1 -> x3, blocking collectives: 15 us -> 48.8 us  [exchange(): lax.all_to_all(rows.reshape(count, 1, lanes), axis, 0, 0, axis_index_grou...]
    all_to_all x2 -> x0, starting transfers between devices: 20.3 us -> none  [exchange(): lax.all_to_all(rows.reshape(count, 1, lanes), axis, 0, 0, axis_index_grou...]
    all_to_all x2 -> x0, waiting for transfers between devices: 9.46 us -> none  [exchange(): lax.all_to_all(rows.reshape(count, 1, lanes), axis, 0, 0, axis_index_grou...]
    pallas_call x6 -> x4, Pallas kernels: 9.43 us -> 5.56 us  [call(): pl.pallas_call(kernel, out_shape=out_shape, in_specs=[space] * len(args),...]
    unnamed x14 -> x12, local copies, waits for them, and re-layouts: 0.63 us -> 0.03 us
  transfers between devices with their start and end apart: 2 -> 0, of which waited for: 2 -> 0; matrix products, arithmetic and copies ran while one was open for 0% -> 0% of each run, Pallas kernels for 8% -> 0%
where the time goes in v4:
time: 55.4 us; the launch traced here: 55.1 us
  blocking collectives  48.8 us (88%)
  Pallas kernels  5.56 us (10%)
  between operations  0.69 us (1%)
    all_to_all x3, blocking collectives, exchange(): lax.all_to_all(rows.reshape(count, 1, lanes), axis, 0, 0, axis_index_grou...  48.8 us
    pallas_call x4, Pallas kernels, call(): pl.pallas_call(kernel, out_shape=out_shape, in_specs=[space] * len(args),...  5.56 us

profile of v4, /device:TPU:56, one launch (start us, length us, event | category | flops | bytes accessed | tf_op | source)
XLA Modules:
  0.0 55.1 jit_solution(6077777718637720151)
XLA Ops:
  0.6 3.1 %shard_map.126 = (f32[448,128]{1,0:T(8,128)S(1)}, f32[8,16,512]{2,1,0:T(8,128)S(1)}, f32[8,16,512]{2,1,0:T(8,128)S(1)}, f32[1,512]{1,0:T(1,128)S(1)}) custom-call(bf16[128,512]{1,0:T(8,128)(2,1)} %key_ref.1, bf16[128,512]{1,0:T(8,128)(2,1)} %value_ref.1, bf16[128,512]{1,0:T(8,128)(2,1)} %gate_ref.1, bf16[128,512]{1,0:T(8,128)(2,1)} %grad_ref.1, ...), custom_call_target="tpu_custom_call" | custom-call | tf_op jit(solution)/shard_map/pallas_call | solution.py:332
  3.7 0.0 copy-start.4
  3.7 0.0 copy-start.5
  3.7 22.8 %all_to_all.15 = f32[448,1,128]{2,1,0:T(1,128)S(1)} all-to-all(f32[448,1,128]{2,1,0:T(1,128)S(1)} %bitcast.18), channel_id=1, replica_groups={{368,376,384,392,400,408,416,424,432,440,448,456,464,472,480,488,496,50..., dimensions={0} | all-to-all | bytes 458752 | tf_op jit(solution)/shard_map/all_to_all | solution.py:344
  26.6 0.0 copy-done.4
  26.6 0.0 copy-done.5
  26.6 0.0 copy-start.3
  26.6 0.1 shard_map.127
  26.7 0.0 copy-start.1
  26.7 0.0 copy-start.2
  26.7 15.1 %all_to_all.16 = f32[320,1,128]{2,1,0:T(1,128)S(1)} all-to-all(f32[320,1,128]{2,1,0:T(1,128)S(1)} %bitcast.17), channel_id=1, replica_groups={{368,376,384,392,400,408,416,424,432,440,448,456,464,472,480,488,496,50..., dimensions={0} | all-to-all | bytes 327680 | tf_op jit(solution)/shard_map/all_to_all | solution.py:344
  41.9 0.0 copy-start
  41.9 10.8 %all_to_all.17 = f32[8,1,128]{2,1,0:T(1,128)S(1)} all-to-all(f32[8,1,128]{2,1,0:T(1,128)S(1)} %bitcast.20), channel_id=1, replica_groups={{261,6,263,0,257,2,259,4},{269,14,271,8,265,10,267,12},{277,22,279,16,2..., dimensions={0} | all-to-all | bytes 8192 | tf_op jit(solution)/shard_map/all_to_all | solution.py:344
  52.7 0.0 copy-done.3
  52.7 0.0 copy-done.1
  52.7 0.0 copy-done.2
  52.7 0.0 copy-done
  52.7 2.3 %shard_map.129 = (bf16[128,512]{1,0:T(8,128)(2,1)}, bf16[128,512]{1,0:T(8,128)(2,1)}, bf16[128,512]{1,0:T(8,128)(2,1)}, bf16[128,512]{1,0:T(8,128)(2,1)}, f32[16...) custom-call(f32[320,128]{1,0:T(8,128)S(1)} %bitcast.15, f32[8,128]{1,0:T(8,128)S(1)} %bitcast.19, ...), custom_call_target="tpu_custom_call" | custom-call | tf_op jit(solution)/shard_map/pallas_call | solution.py:332
  (1 shorter events, 0.0 us)
Async XLA Ops:
  3.7 22.9 %copy-start.4 = (f32[16,512]{1,0:T(8,128)S(1)}, f32[16,512]{1,0:T(8,128)}, u32[]{:S(2)}) copy-start(f32[16,512]{1,0:T(8,128)} %rate_ref.3) | copy-start | bytes 98308
  3.7 22.9 %copy-start.5 = (f32[16,512]{1,0:T(8,128)S(1)}, f32[16,512]{1,0:T(8,128)}, u32[]{:S(2)}) copy-start(f32[16,512]{1,0:T(8,128)} %res_ref.3) | copy-start | bytes 98308
  26.6 26.1 %copy-start.3 = (bf16[128,512]{1,0:T(8,128)(2,1)S(1)}, bf16[128,512]{1,0:T(8,128)(2,1)}, u32[]{:S(2)}) copy-start(bf16[128,512]{1,0:T(8,128)(2,1)} %grad_ref.1) | copy-start | bytes 393220
  26.7 26.0 %copy-start.1 = (bf16[128,512]{1,0:T(8,128)(2,1)S(1)}, bf16[128,512]{1,0:T(8,128)(2,1)}, u32[]{:S(2)}) copy-start(bf16[128,512]{1,0:T(8,128)(2,1)} %value_ref.1) | copy-start | bytes 393220
  26.7 26.0 %copy-start.2 = (bf16[128,512]{1,0:T(8,128)(2,1)S(1)}, bf16[128,512]{1,0:T(8,128)(2,1)}, u32[]{:S(2)}) copy-start(bf16[128,512]{1,0:T(8,128)(2,1)} %gate_ref.1) | copy-start | bytes 393220
  41.9 10.9 %copy-start = (bf16[128,512]{1,0:T(8,128)(2,1)S(1)}, bf16[128,512]{1,0:T(8,128)(2,1)}, u32[]{:S(2)}) copy-start(bf16[128,512]{1,0:T(8,128)(2,1)} %key_ref.1) | copy-start | bytes 393220

commit v5 on v4

--- a/solution.py
+++ b/solution.py
@@ -13,7 +13,7 @@
 ROWS_OUT = 7
 ROWS_BACK = 5
 Y_RUN = 4
-LEAD = 46
+LEADS = (47, 31)
 ROOT_HIGH = 5
 PART = 16
 GROUPS_AT_ONCE = 2
@@ -112,11 +112,14 @@
     return jnp.where(keep, moved, 0.0)
 
 
-def scan_kernel(block, modes, lead, in_ref, res_ref, rate_ref, out_ref):
+def scan_kernel(block, modes, in_ref, res_ref, rate_ref, out_ref):
     chunk = SUBLANES
-    turn, cut = divmod(-lead % (chunk * SUBLANES), chunk)
+    blocks = chunk * SUBLANES
+    upper = lax.rem(lax.axis_index("chan"), 2)
+    (low_turn, cut), (high_turn, _) = (divmod(-lead % blocks, chunk) for lead in LEADS)
+    turn = jnp.where(upper == 1, high_turn, low_turn)
+    lead = jnp.where(upper == 1, LEADS[1], LEADS[0])
     seam = lax.broadcasted_iota(jnp.int32, (SUBLANES, LANES), 0) == turn
-    blocks = chunk * SUBLANES
     place = lax.rem(lax.axis_index("seq") + (blocks - lead), blocks)
     own_mode, own_group = lax.rem(place, modes), lax.div(place, modes)
     rows = lax.broadcasted_iota(jnp.int32, (modes, LANES), 0)
@@ -153,8 +156,8 @@
         back = decay * back + load(v, 2)
         if v == cut:
             back = jnp.where(seam, 0.0, back)
-    state, timed = (pltpu.roll(value, -turn % SUBLANES, 0) for value in (state, timed))
-    back = pltpu.roll(back, (SUBLANES - 1 - turn) % SUBLANES, 0)
+    state, timed = (pltpu.roll(value, SUBLANES - turn, 0) for value in (state, timed))
+    back = pltpu.roll(back, SUBLANES - 1 - turn, 0)
     span = block * chunk
     distance = 1
     while distance < SUBLANES:
@@ -164,7 +167,7 @@
         state = state + older
         back = back + far * shifted(back, -distance)
         distance *= 2
-    state, timed = (pltpu.roll(value, (turn + 1) % SUBLANES, 0) for value in (state, timed))
+    state, timed = (pltpu.roll(value, turn + 1, 0) for value in (state, timed))
     back = pltpu.roll(back, turn, 0)
     start_state, start_timed = jnp.where(seam, 0.0, state), jnp.where(seam, 0.0, timed)
     end_back = jnp.where(seam, 0.0, back)
@@ -404,16 +407,15 @@
     groups = width // LANES
     owners = groups * modes
     assert owners == blocks
-    order = [(LEAD + at) % blocks for at in range(blocks)]
-
+    orders = [[(LEADS[shard % 2] + at) % blocks * shards + shard for at in range(blocks)] for shard in range(shards)]
     sent, ahead, behind, skip_row = summarize(key_in, value_in, gate_in, out_grad, log_rate, skip.reshape(1, width))
-    arrived = exchange(sent, "seq", [order])
+    arrived = exchange(sent, ("seq", "chan"), orders)
     reply = call(
-        functools.partial(scan_kernel, block, modes, LEAD),
+        functools.partial(scan_kernel, block, modes),
         floats(blocks * ROWS_BACK, LANES),
         arrived, residue, log_rate,
     )
-    states = exchange(reply, "seq", [order])
+    states = exchange(reply, ("seq", "chan"), orders)
     raw_res, raw_log, raw_skip, squares = call(
         functools.partial(square_kernel, modes),
         (floats(modes, width), floats(modes, width), floats(1, width), floats(shards, LANES)),

time: 55.4 us -> 54.1 us (0.977)
  blocking collectives: 48.8 us -> 47.5 us
    all_to_all x3, blocking collectives: 48.8 us -> 47.5 us  [exchange(): lax.all_to_all(rows.reshape(count, 1, lanes), axis, 0, 0, axis_index_grou...]
where the time goes in v5:
time: 54.1 us; the launch traced here: 53.8 us
  blocking collectives  47.5 us (88%)
  Pallas kernels  5.56 us (10%)
  between operations  0.69 us (1%)
    all_to_all x3, blocking collectives, exchange(): lax.all_to_all(rows.reshape(count, 1, lanes), axis, 0, 0, axis_index_grou...  47.5 us
    pallas_call x4, Pallas kernels, call(): pl.pallas_call(kernel, out_shape=out_shape, in_specs=[space] * len(args),...  5.56 us

profile of v5, /device:TPU:56, one launch (start us, length us, event | category | flops | bytes accessed | tf_op | source)
XLA Modules:
  0.0 53.8 jit_solution(6555813980245189127)
XLA Ops:
  0.6 3.1 %shard_map.126 = (f32[448,128]{1,0:T(8,128)S(1)}, f32[8,16,512]{2,1,0:T(8,128)S(1)}, f32[8,16,512]{2,1,0:T(8,128)S(1)}, f32[1,512]{1,0:T(1,128)S(1)}) custom-call(bf16[128,512]{1,0:T(8,128)(2,1)} %key_ref.1, bf16[128,512]{1,0:T(8,128)(2,1)} %value_ref.1, bf16[128,512]{1,0:T(8,128)(2,1)} %gate_ref.1, bf16[128,512]{1,0:T(8,128)(2,1)} %grad_ref.1, ...), custom_call_target="tpu_custom_call" | custom-call | tf_op jit(solution)/shard_map/pallas_call | solution.py:335
  3.7 0.0 copy-start.4
  3.7 0.0 copy-start.5
  3.7 21.9 %all_to_all.15 = f32[448,1,128]{2,1,0:T(1,128)S(1)} all-to-all(f32[448,1,128]{2,1,0:T(1,128)S(1)} %bitcast.18), channel_id=1, replica_groups={{376,384,392,400,408,416,424,432,440,448,456,464,472,480,488,496,504,0,..., dimensions={0} | all-to-all | bytes 458752 | tf_op jit(solution)/shard_map/all_to_all | solution.py:347
  25.6 0.0 copy-done.4
  25.6 0.0 copy-done.5
  25.6 0.0 copy-start.3
  25.6 0.1 shard_map.127
  25.7 0.0 copy-start.1
  25.8 0.0 copy-start.2
  25.8 14.8 %all_to_all.16 = f32[320,1,128]{2,1,0:T(1,128)S(1)} all-to-all(f32[320,1,128]{2,1,0:T(1,128)S(1)} %bitcast.17), channel_id=1, replica_groups={{376,384,392,400,408,416,424,432,440,448,456,464,472,480,488,496,504,0,..., dimensions={0} | all-to-all | bytes 327680 | tf_op jit(solution)/shard_map/all_to_all | solution.py:347
  40.6 0.0 copy-start
  40.6 10.8 %all_to_all.17 = f32[8,1,128]{2,1,0:T(1,128)S(1)} all-to-all(f32[8,1,128]{2,1,0:T(1,128)S(1)} %bitcast.20), channel_id=1, replica_groups={{261,6,263,0,257,2,259,4},{269,14,271,8,265,10,267,12},{277,22,279,16,2..., dimensions={0} | all-to-all | bytes 8192 | tf_op jit(solution)/shard_map/all_to_all | solution.py:347
  51.5 0.0 copy-done.3
  51.5 0.0 copy-done.1
  51.5 0.0 copy-done.2
  51.5 0.0 copy-done
  51.5 2.3 %shard_map.129 = (bf16[128,512]{1,0:T(8,128)(2,1)}, bf16[128,512]{1,0:T(8,128)(2,1)}, bf16[128,512]{1,0:T(8,128)(2,1)}, bf16[128,512]{1,0:T(8,128)(2,1)}, f32[16...) custom-call(f32[320,128]{1,0:T(8,128)S(1)} %bitcast.15, f32[8,128]{1,0:T(8,128)S(1)} %bitcast.19, ...), custom_call_target="tpu_custom_call" | custom-call | tf_op jit(solution)/shard_map/pallas_call | solution.py:335
  (1 shorter events, 0.0 us)
Async XLA Ops:
  3.7 21.9 %copy-start.4 = (f32[16,512]{1,0:T(8,128)S(1)}, f32[16,512]{1,0:T(8,128)}, u32[]{:S(2)}) copy-start(f32[16,512]{1,0:T(8,128)} %rate_ref.3) | copy-start | bytes 98308
  3.7 21.9 %copy-start.5 = (f32[16,512]{1,0:T(8,128)S(1)}, f32[16,512]{1,0:T(8,128)}, u32[]{:S(2)}) copy-start(f32[16,512]{1,0:T(8,128)} %res_ref.3) | copy-start | bytes 98308
  25.6 25.8 %copy-start.3 = (bf16[128,512]{1,0:T(8,128)(2,1)S(1)}, bf16[128,512]{1,0:T(8,128)(2,1)}, u32[]{:S(2)}) copy-start(bf16[128,512]{1,0:T(8,128)(2,1)} %grad_ref.1) | copy-start | bytes 393220
  25.7 25.7 %copy-start.1 = (bf16[128,512]{1,0:T(8,128)(2,1)S(1)}, bf16[128,512]{1,0:T(8,128)(2,1)}, u32[]{:S(2)}) copy-start(bf16[128,512]{1,0:T(8,128)(2,1)} %value_ref.1) | copy-start | bytes 393220
  25.8 25.7 %copy-start.2 = (bf16[128,512]{1,0:T(8,128)(2,1)S(1)}, bf16[128,512]{1,0:T(8,128)(2,1)}, u32[]{:S(2)}) copy-start(bf16[128,512]{1,0:T(8,128)(2,1)} %gate_ref.1) | copy-start | bytes 393220
  40.6 10.9 %copy-start = (bf16[128,512]{1,0:T(8,128)(2,1)S(1)}, bf16[128,512]{1,0:T(8,128)(2,1)}, u32[]{:S(2)}) copy-start(bf16[128,512]{1,0:T(8,128)(2,1)} %key_ref.1) | copy-start | bytes 393220

commit v6 on v5

--- a/solution.py
+++ b/solution.py
@@ -21,15 +21,16 @@
 PARAMS = pltpu.CompilerParams(vmem_limit_bytes=32 * 1024 * 1024)
 
 
-def tile_of(ref, chunk, group):
-    return ref[pl.ds(pl.multiple_of(chunk * SUBLANES, SUBLANES), SUBLANES), group * LANES : (group + 1) * LANES]
+def tile_of(ref, part, piece, group):
+    row = part * (PART + SUBLANES) + (piece + 1) * SUBLANES
+    return ref[group, pl.ds(pl.multiple_of(row, SUBLANES), SUBLANES), :]
 
 
 def spread(tile, row):
     return jnp.broadcast_to(tile[row : row + 1], (SUBLANES, LANES))
 
 
-def summary_kernel(key_hbm, value_hbm, gate_hbm, grad_hbm, rate_hbm, skip_hbm, out_ref, ahead_ref, behind_ref, skip_ref, key_ref, value_ref, gate_ref, grad_ref, rate_ref, mixed, slope, sems):
+def summary_kernel(key_hbm, value_hbm, gate_hbm, grad_hbm, rate_hbm, skip_hbm, out_ref, ahead_ref, behind_ref, skip_ref, mixed, slope, key_ref, value_ref, gate_ref, grad_ref, rate_ref, sems):
     block, width = key_ref.shape
     modes = rate_ref.shape[0]
     halves, groups = modes // SUBLANES, width // LANES
@@ -45,12 +46,23 @@
             steps[half, group] = jnp.exp(-rate)
     copies[1].wait()
     copies[2].wait()
-    mixed[...] = key_ref[...].astype(jnp.float32) * value_ref[...].astype(jnp.float32)
+    zero = jnp.zeros((SUBLANES, LANES), jnp.float32)
+
+    def fill(target, one_ref, other_ref):
+        for group in range(groups):
+            lanes = slice(group * LANES, (group + 1) * LANES)
+            for part in range(block // PART):
+                at, rows = part * (PART + SUBLANES), slice(part * PART, (part + 1) * PART)
+                target[group, at : at + SUBLANES, :] = zero
+                product = one_ref[rows, lanes].astype(jnp.float32) * other_ref[rows, lanes].astype(jnp.float32)
+                target[group, at + SUBLANES : at + SUBLANES + PART, :] = product
+            target[group, block // PART * (PART + SUBLANES) :, :] = zero
+
+    fill(mixed, key_ref, value_ref)
     copies[3].wait()
     copies[4].wait()
-    slope[...] = grad_ref[...].astype(jnp.float32) * gate_ref[...].astype(jnp.float32)
+    fill(slope, grad_ref, gate_ref)
     copies[5].wait()
-    zero = jnp.zeros((SUBLANES, LANES), jnp.float32)
     for first in range(0, groups, GROUPS_AT_ONCE):
         held = range(first, first + GROUPS_AT_ONCE)
         keys = [(half, group) for half in range(halves) for group in held]
@@ -63,10 +75,10 @@
                 ahead_ref[part, rows, lanes] = carry[at][0]
                 behind_ref[block // PART - 1 - part, rows, lanes] = carry[at][4]
             for piece in range(PART // SUBLANES):
-                chunk = part * (PART // SUBLANES) + piece
-                x_tiles = {group: tile_of(mixed, chunk, group) for group in held}
-                z_tiles = {group: tile_of(slope, chunk, group) for group in held}
-                back_tiles = {group: tile_of(slope, block // SUBLANES - 1 - chunk, group) for group in held}
+                x_tiles = {group: tile_of(mixed, part, piece, group) for group in held}
+                z_tiles = {group: tile_of(slope, part, piece, group) for group in held}
+                mirror = block // PART - 1 - part, PART // SUBLANES - 1 - piece
+                back_tiles = {group: tile_of(slope, *mirror, group) for group in held}
                 for inner in range(SUBLANES):
                     x_rows = {group: spread(x_tiles[group], inner) for group in held}
                     z_rows = {group: spread(z_tiles[group], inner) for group in held}
@@ -90,8 +102,7 @@
             state, timed, plain_sum, timed_sum, back, back_timed = done[at]
             step = steps[half, group]
             base = (group * modes + half * SUBLANES) * ROWS_OUT
-            lanes = slice(group * LANES, (group + 1) * LANES)
-            skip_part = jnp.sum(mixed[:, lanes] * slope[:, lanes], axis=0, keepdims=True)
+            skip_part = jnp.sum(mixed[group] * slope[group], axis=0, keepdims=True)
             rows = (
                 step * state,
                 step * (timed + state),
@@ -213,7 +224,7 @@
     out_ref[...] = jnp.broadcast_to(jnp.sum(total, axis=0, keepdims=True), out_ref.shape)
 
 
-def output_kernel(count, in_ref, squares_ref, raw_res_ref, raw_log_ref, raw_skip_ref, ahead_ref, behind_ref, key_ref, value_ref, gate_ref, grad_ref, res_ref, rate_ref, skip_ref, out_hbm, gate_hbm, key_hbm, value_hbm, res_hbm, log_hbm, gain_hbm, out_ref, gate_out, key_out, value_out, mixed, slope, entering, leaving, taps, res_out, log_out, gain_out, sems, clip_sems):
+def output_kernel(count, in_ref, squares_ref, raw_res_ref, raw_log_ref, raw_skip_ref, ahead_ref, behind_ref, mixed_ref, slope_ref, key_ref, value_ref, gate_ref, grad_ref, res_ref, rate_ref, skip_ref, out_hbm, gate_hbm, key_hbm, value_hbm, res_hbm, log_hbm, gain_hbm, out_ref, gate_out, key_out, value_out, entering, leaving, taps, res_out, log_out, gain_out, sems, clip_sems):
     block, width = key_ref.shape
     modes = rate_ref.shape[0]
     groups = width // LANES
@@ -244,15 +255,7 @@
 
     for group in range(groups):
         lanes = slice(group * LANES, (group + 1) * LANES)
-        for part in range(parts):
-            at, rows = part * (PART + SUBLANES), slice(part * PART, (part + 1) * PART)
-            for ref in (mixed, slope):
-                ref[at : at + SUBLANES, :] = zero
-            start = at + SUBLANES
-            mixed[start : start + PART, :] = key_ref[rows, lanes].astype(jnp.float32) * value_ref[rows, lanes].astype(jnp.float32)
-            slope[start : start + PART, :] = grad_ref[rows, lanes].astype(jnp.float32) * gate_ref[rows, lanes].astype(jnp.float32)
-        for ref in (mixed, slope):
-            ref[parts * (PART + SUBLANES) :, :] = zero
+        mixed, slope = mixed_ref.at[group], slope_ref.at[group]
         powers = []
         for half in range(halves):
             rows = slice(half * SUBLANES, (half + 1) * SUBLANES)
@@ -372,26 +375,26 @@
             floats(block // PART, modes, width),
             floats(block // PART, modes, width),
             floats(1, width),
+            floats(width // LANES, block // PART * (PART + SUBLANES) + SUBLANES, LANES),
+            floats(width // LANES, block // PART * (PART + SUBLANES) + SUBLANES, LANES),
         ),
         *in_hbm(key_in, value_in, gate_in, out_grad, log_rate, skip),
         scratch=[pltpu.VMEM((block, width), jnp.bfloat16)] * 4
         + [pltpu.VMEM((modes, width), jnp.float32)]
-        + [pltpu.VMEM((block, width), jnp.float32)] * 2
         + [pltpu.SemaphoreType.DMA((6,))],
         space=pl.BlockSpec(memory_space=pltpu.HBM),
     )
 
 
-def finish(states, squares, raw_res, raw_log, raw_skip, ahead, behind, key_in, value_in, gate_in, out_grad, residue, log_rate, skip_row):
+def finish(states, squares, raw_res, raw_log, raw_skip, ahead, behind, mixed, slope, key_in, value_in, gate_in, out_grad, residue, log_rate, skip_row):
     block, width = key_in.shape
     modes, groups, shards = residue.shape[0], width // LANES, squares.shape[0]
     return call(
         functools.partial(output_kernel, float((2 * modes + 1) * width * shards)),
         (jax.ShapeDtypeStruct((block, width), jnp.bfloat16),) * 4 + (floats(modes, width), floats(modes, width), floats(1, width)),
-        states, squares, raw_res, raw_log, raw_skip, ahead, behind, key_in, value_in, gate_in, out_grad, residue, log_rate, skip_row,
+        states, squares, raw_res, raw_log, raw_skip, ahead, behind, mixed, slope, key_in, value_in, gate_in, out_grad, residue, log_rate, skip_row,
         out_space=pl.BlockSpec(memory_space=pl.ANY),
         scratch=[pltpu.VMEM((block, width), jnp.bfloat16)] * 4
-        + [pltpu.VMEM((block // PART * (PART + SUBLANES) + SUBLANES, LANES), jnp.float32)] * 2
         + [pltpu.VMEM((block // PART * modes, LANES), jnp.float32)] * 2
         + [pltpu.VMEM((PART, LANES), jnp.float32)]
         + [pltpu.VMEM((modes, width), jnp.float32)] * 2
@@ -408,7 +411,7 @@
     owners = groups * modes
     assert owners == blocks
     orders = [[(LEADS[shard % 2] + at) % blocks * shards + shard for at in range(blocks)] for shard in range(shards)]
-    sent, ahead, behind, skip_row = summarize(key_in, value_in, gate_in, out_grad, log_rate, skip.reshape(1, width))
+    sent, ahead, behind, skip_row, mixed, slope = summarize(key_in, value_in, gate_in, out_grad, log_rate, skip.reshape(1, width))
     arrived = exchange(sent, ("seq", "chan"), orders)
     reply = call(
         functools.partial(scan_kernel, block, modes),
@@ -423,7 +426,7 @@
     )
     squares = exchange(squares, ("seq", "chan"), near_groups(blocks, shards))
     gated_out, gate_grad, key_grad, value_grad, residue_grad, log_rate_grad, skip_grad = finish(
-        states, squares, raw_res, raw_log, raw_skip, ahead, behind, key_in, value_in, gate_in, out_grad, residue, log_rate, skip_row
+        states, squares, raw_res, raw_log, raw_skip, ahead, behind, mixed, slope, key_in, value_in, gate_in, out_grad, residue, log_rate, skip_row
     )
     return gated_out, gate_grad, key_grad, value_grad, residue_grad, log_rate_grad, skip_grad.reshape(width)
 

time: 54.1 us -> 54 us (level)
  no operation moved by 1% of the time
where the time goes in v6:
time: 54 us; the launch traced here: 53.7 us
  blocking collectives  47.5 us (88%)
  Pallas kernels  5.5 us (10%)
  between operations  0.69 us (1%)
    all_to_all x3, blocking collectives, exchange(): lax.all_to_all(rows.reshape(count, 1, lanes), axis, 0, 0, axis_index_grou...  47.5 us
    pallas_call x4, Pallas kernels, call(): pl.pallas_call(kernel, out_shape=out_shape, in_specs=[space] * len(args),...  5.5 us

profile of v6, /device:TPU:56, one launch (start us, length us, event | category | flops | bytes accessed | tf_op | source)
XLA Modules:
  0.0 53.7 jit_solution(5752309607064112334)
XLA Ops:
  0.6 3.1 %shard_map.126 = (f32[448,128]{1,0:T(8,128)S(1)}, f32[8,16,512]{2,1,0:T(8,128)S(1)}, f32[8,16,512]{2,1,0:T(8,128)S(1)}, f32[1,512]{1,0:T(1,128)S(1)}, f32[4,200,...) custom-call(bf16[128,512]{1,0:T(8,128)(2,1)} %key_ref.1, bf16[128,512]{1,0:T(8,128)(2,1)} %value_ref.1, ...), custom_call_target="tpu_custom_call" | custom-call | tf_op jit(solution)/shard_map/pallas_call | solution.py:338
  3.8 0.0 copy-start.4
  3.8 0.0 copy-start.5
  3.8 21.9 %all_to_all.15 = f32[448,1,128]{2,1,0:T(1,128)S(1)} all-to-all(f32[448,1,128]{2,1,0:T(1,128)S(1)} %bitcast.18), channel_id=1, replica_groups={{376,384,392,400,408,416,424,432,440,448,456,464,472,480,488,496,504,0,..., dimensions={0} | all-to-all | bytes 458752 | tf_op jit(solution)/shard_map/all_to_all | solution.py:350
  25.6 0.0 copy-done.4
  25.7 0.0 copy-done.5
  25.7 0.0 copy-start.3
  25.7 0.1 shard_map.127
  25.8 0.0 copy-start.1
  25.8 0.0 copy-start.2
  25.8 14.8 %all_to_all.16 = f32[320,1,128]{2,1,0:T(1,128)S(1)} all-to-all(f32[320,1,128]{2,1,0:T(1,128)S(1)} %bitcast.17), channel_id=1, replica_groups={{376,384,392,400,408,416,424,432,440,448,456,464,472,480,488,496,504,0,..., dimensions={0} | all-to-all | bytes 327680 | tf_op jit(solution)/shard_map/all_to_all | solution.py:350
  40.6 0.0 copy-start
  40.7 10.8 %all_to_all.17 = f32[8,1,128]{2,1,0:T(1,128)S(1)} all-to-all(f32[8,1,128]{2,1,0:T(1,128)S(1)} %bitcast.20), channel_id=1, replica_groups={{261,6,263,0,257,2,259,4},{269,14,271,8,265,10,267,12},{277,22,279,16,2..., dimensions={0} | all-to-all | bytes 8192 | tf_op jit(solution)/shard_map/all_to_all | solution.py:350
  51.5 0.0 copy-done.3
  51.5 0.0 copy-done.1
  51.5 0.0 copy-done.2
  51.5 0.0 copy-done
  51.5 2.2 %shard_map.129 = (bf16[128,512]{1,0:T(8,128)(2,1)}, bf16[128,512]{1,0:T(8,128)(2,1)}, bf16[128,512]{1,0:T(8,128)(2,1)}, bf16[128,512]{1,0:T(8,128)(2,1)}, f32[16...) custom-call(f32[320,128]{1,0:T(8,128)S(1)} %bitcast.15, f32[8,128]{1,0:T(8,128)S(1)} %bitcast.19, ...), custom_call_target="tpu_custom_call" | custom-call | tf_op jit(solution)/shard_map/pallas_call | solution.py:338
  (1 shorter events, 0.0 us)
Async XLA Ops:
  3.8 21.9 %copy-start.4 = (f32[16,512]{1,0:T(8,128)S(1)}, f32[16,512]{1,0:T(8,128)}, u32[]{:S(2)}) copy-start(f32[16,512]{1,0:T(8,128)} %rate_ref.3) | copy-start | bytes 98308
  3.8 21.9 %copy-start.5 = (f32[16,512]{1,0:T(8,128)S(1)}, f32[16,512]{1,0:T(8,128)}, u32[]{:S(2)}) copy-start(f32[16,512]{1,0:T(8,128)} %res_ref.3) | copy-start | bytes 98308
  25.7 25.8 %copy-start.3 = (bf16[128,512]{1,0:T(8,128)(2,1)S(1)}, bf16[128,512]{1,0:T(8,128)(2,1)}, u32[]{:S(2)}) copy-start(bf16[128,512]{1,0:T(8,128)(2,1)} %grad_ref.1) | copy-start | bytes 393220
  25.8 25.7 %copy-start.1 = (bf16[128,512]{1,0:T(8,128)(2,1)S(1)}, bf16[128,512]{1,0:T(8,128)(2,1)}, u32[]{:S(2)}) copy-start(bf16[128,512]{1,0:T(8,128)(2,1)} %value_ref.1) | copy-start | bytes 393220
  25.8 25.7 %copy-start.2 = (bf16[128,512]{1,0:T(8,128)(2,1)S(1)}, bf16[128,512]{1,0:T(8,128)(2,1)}, u32[]{:S(2)}) copy-start(bf16[128,512]{1,0:T(8,128)(2,1)} %gate_ref.1) | copy-start | bytes 393220
  40.6 10.9 %copy-start = (bf16[128,512]{1,0:T(8,128)(2,1)S(1)}, bf16[128,512]{1,0:T(8,128)(2,1)}, u32[]{:S(2)}) copy-start(bf16[128,512]{1,0:T(8,128)(2,1)} %key_ref.1) | copy-start | bytes 393220
